TPU v7x, 256 devices: a whole 4x4x8 slice. The times are simulated.
256 devices in a mesh: seq: 16 (over y_hi, z), dp: 16 (over y_lo, x, core).
Axes of the slice: x: 4, y: 4 (y_hi: 2, y_lo: 2; y = y_hi * 2 + y_lo), z: 8, core: 2. Of those that a mesh axis runs over, the one named last changes fastest.
Arguments:
- byte_ids: int32 [16, 4096], P('dp', 'seq'), may hold values from 0 to 255
- embedding: bfloat16 [256, 1024], replicated, may hold values from -6 to 6
- gain: float32 [1024], replicated, may hold values from 0.5 to 1.5
- w_query: bfloat16 [1024, 1024], replicated, may hold values from -2 to 2
- w_key: bfloat16 [1024, 1024], replicated, may hold values from -2 to 2
- w_value: bfloat16 [1024, 1024], replicated, may hold values from -0.1875 to 0.1875
- w_out: bfloat16 [1024, 1024], replicated, may hold values from -0.1875 to 0.1875
- d_output: bfloat16 [16, 4096, 1024], P('dp', 'seq'), may hold values from -0.03125 to 0.03125
Outputs:
- d_key_weight: float32 [1024, 1024], P(('seq', 'dp'))
- d_gain: float32 [1024], P(('seq', 'dp'))
- d_embedding: float32 [256, 1024], P(('seq', 'dp'))
All inputs are finite; a program needn't handle non-finite values.
Results may differ from a plain program's by a relative error of at most 0.0083.
Values may be sent and summed in bfloat16 or wider, within the bound.
No kernel may reach another device: no remote copies, remote signals or barrier semaphores. Data moves between devices by JAX's collectives and lax.ppermute only.
A program may use at most 128 MiB of HBM per device.

v0:
```python
import jax
import jax.numpy as jnp
from jax import lax
from jax.sharding import PartitionSpec as P

HEADS = 8


NEGATIVE = -1e30
EPSILON = 1e-05
THETA = 10000.0


def shifted(value, axis, steps):
    count = lax.axis_size(axis)
    initial, last = (max(0, -steps), min(count, count - steps))
    return lax.ppermute(value, axis, [(source, source + steps) for source in range(initial, last)])


def tables(position, half_dim):
    inverse = THETA ** (-jnp.arange(half_dim, dtype=jnp.float32) / half_dim)
    angles = position.astype(jnp.float32)[:, None] * inverse[None, :]
    return (jnp.cos(angles), jnp.sin(angles))


def rotate(matrix, cosine, sine_table, head_count, direction):
    row_count = matrix.shape[0]
    per_head = matrix.reshape(row_count, head_count, -1)
    half_dim = per_head.shape[-1] // 2
    former = per_head[..., :half_dim]
    latter = per_head[..., half_dim:]
    cos_part = cosine[:, None, :]
    sin_part = direction * sine_table[:, None, :]
    joined = jnp.concatenate(
        [former * cos_part - latter * sin_part, latter * cos_part + former * sin_part], axis=-1
    )
    return joined.reshape(row_count, -1)


def product(left_op, right_op):
    return jnp.dot(left_op, right_op, preferred_element_type=jnp.float32)


def contract(left_op, right_op):
    return lax.dot_general(
        left_op, right_op, (((0,), (0,)), ((), ())), preferred_element_type=jnp.float32
    )


def against(left_op, right_op):
    return lax.dot_general(
        left_op, right_op, (((1,), (1,)), ((), ())), preferred_element_type=jnp.float32
    )


def band_attention(queries, key_cat, value_cat, grad_out, w_out, leading, head_count):
    row_count, feat_width = queries.shape
    head_dim = feat_width // head_count
    score_scale = head_dim ** (-0.5)
    query_h = queries.reshape(row_count, head_count, head_dim)
    key_h = key_cat.reshape(2 * row_count, head_count, head_dim)
    value_h = value_cat.reshape(2 * row_count, head_count, head_dim)
    scores = (
        jnp.einsum("qhd,khd->hqk", query_h, key_h, preferred_element_type=jnp.float32) * score_scale
    )
    row_pos = jnp.arange(row_count, dtype=jnp.int32)[:, None]
    col_pos = jnp.arange(2 * row_count, dtype=jnp.int32)[None, :]
    allowed = (
        (col_pos > row_pos)
        & (col_pos <= row_pos + row_count)
        & ((col_pos >= row_count) | jnp.logical_not(leading))
    )
    scores = jnp.where(allowed[None], scores, NEGATIVE)
    highest = jnp.max(scores, axis=-1, keepdims=True)
    weights = jnp.exp(scores - highest)
    probability = weights / jnp.sum(weights, axis=-1, keepdims=True)
    rounded = probability.astype(jnp.bfloat16)
    grad_att = product(grad_out, w_out).astype(jnp.bfloat16)
    grad_h = grad_att.reshape(row_count, head_count, head_dim)
    grad_probs = jnp.einsum("qhd,khd->hqk", grad_h, value_h, preferred_element_type=jnp.float32)
    grad_values = jnp.einsum(
        "hqk,qhd->khd", rounded, grad_h, preferred_element_type=jnp.float32
    ).reshape(2 * row_count, feat_width)
    row_delta = jnp.sum(probability * grad_probs, axis=-1, keepdims=True)
    grad_scores = (probability * (grad_probs - row_delta) * score_scale).astype(jnp.bfloat16)
    grad_queries = jnp.einsum(
        "hqk,khd->qhd", grad_scores, key_h, preferred_element_type=jnp.float32
    ).reshape(row_count, feat_width)
    grad_keys = jnp.einsum(
        "hqk,qhd->khd", grad_scores, query_h, preferred_element_type=jnp.float32
    ).reshape(2 * row_count, feat_width)
    return (grad_queries, grad_keys, grad_values)


def local(byte_ids, embedding, gain, w_query, w_key, w_value, w_out, d_output):
    byte_row = byte_ids[0]
    grad_row = d_output[0]
    row_count = byte_row.shape[0]
    hd_width = w_query.shape[1]
    head_count = HEADS
    half_dim = hd_width // head_count // 2
    vocab_size = embedding.shape[0]
    block_index = lax.axis_index("seq")
    one_hot = (byte_row[:, None] == jnp.arange(vocab_size, dtype=jnp.int32)[None, :]).astype(
        jnp.bfloat16
    )
    inputs = product(one_hot, embedding)
    recip = lax.rsqrt(jnp.mean(inputs * inputs, axis=-1, keepdims=True) + EPSILON)
    normed = (inputs * recip * gain[None, :]).astype(jnp.bfloat16)
    places = block_index * row_count + jnp.arange(row_count, dtype=jnp.int32)
    cosine, sine_table = tables(places, half_dim)
    prev_cos, prev_sin = tables(places - row_count, half_dim)
    queries = rotate(product(normed, w_query), cosine, sine_table, head_count, 1.0).astype(
        jnp.bfloat16
    )
    keys_here = rotate(product(normed, w_key), cosine, sine_table, head_count, 1.0).astype(
        jnp.bfloat16
    )
    values_here = product(normed, w_value).astype(jnp.bfloat16)
    moved = shifted(jnp.stack([keys_here, values_here]), "seq", 1)
    key_prev = moved[0]
    value_prev = moved[1]
    grad_q, grad_k, grad_v = band_attention(
        queries,
        jnp.concatenate([key_prev, keys_here], axis=0),
        jnp.concatenate([value_prev, values_here], axis=0),
        grad_row,
        w_out,
        block_index == 0,
        head_count,
    )
    grad_query = rotate(grad_q, cosine, sine_table, head_count, -1.0).astype(jnp.bfloat16)
    key_own = rotate(grad_k[row_count:], cosine, sine_table, head_count, -1.0).astype(jnp.bfloat16)
    key_next = rotate(grad_k[:row_count], prev_cos, prev_sin, head_count, -1.0).astype(jnp.bfloat16)
    value_own = grad_v[row_count:].astype(jnp.bfloat16)
    value_next = grad_v[:row_count].astype(jnp.bfloat16)
    grad_wk = contract(normed, key_own)
    grad_normed = (
        against(grad_query, w_query) + against(key_own, w_key) + against(value_own, w_value)
    )
    moved_back = shifted(jnp.stack([key_next, value_next]), "seq", -1)
    key_from = moved_back[0]
    value_from = moved_back[1]
    grad_wk = grad_wk + contract(normed, key_from)
    grad_normed = grad_normed + against(key_from, w_key) + against(value_from, w_value)
    scaled = inputs * recip
    grad_gain = jnp.sum(grad_normed * scaled, axis=0)
    grad_scaled = grad_normed * gain[None, :]
    grad_inputs = recip * grad_scaled - inputs * recip**3 * jnp.mean(
        grad_scaled * inputs, axis=-1, keepdims=True
    )
    grad_table = lax.dot_general(
        one_hot.astype(jnp.float32),
        grad_inputs,
        (((0,), (0,)), ((), ())),
        precision=lax.Precision.HIGHEST,
        preferred_element_type=jnp.float32,
    )
    summed = (
        lax.psum_scatter(grad_wk, ("seq", "dp"), scatter_dimension=0, tiled=True),
        lax.psum_scatter(grad_gain, ("seq", "dp"), scatter_dimension=0, tiled=True),
        lax.psum_scatter(grad_table, ("seq", "dp"), scatter_dimension=0, tiled=True),
    )
    return (summed[0], summed[1], summed[2])


def solution(mesh):
    in_specs = (P("dp", "seq"), P(), P(), P(), P(), P(), P(), P("dp", "seq", None))
    out_specs = (P(("seq", "dp"), None), P(("seq", "dp")), P(("seq", "dp"), None))
    return jax.shard_map(local, mesh=mesh, in_specs=in_specs, out_specs=out_specs, check_vma=False)
```

profile of v0, /device:TPU:1, one launch (start us, length us, event | category | flops | bytes accessed | tf_op | source)
XLA Modules:
  0.0 443.0 jit_solution(3079951659959602599)
XLA Ops:
  7.2 0.0 copy-start
  7.2 0.0 all-reduce.6.cloned.1.call-start
  7.2 1.6 multiply_reduce_fusion.3
  8.9 0.8 multiply_convert_fusion.1
  9.7 0.8 copy-done.1
  10.5 0.7 convolution_bitcast_fusion
  11.3 0.2 copy.70
  11.5 1.7 fusion.69
  13.1 1.7 multiply_cosine_fusion
  14.9 1.9 multiply_subtract_fusion
  16.8 0.3 maximum_convert_fusion
  17.1 0.8 copy-done.7
  17.9 1.2 copy.46
  19.1 2.1 convert_element_type.84
  21.2 2.6 convolution_convert_fusion.1
  23.8 2.3 pad_maximum_fusion
  26.1 5.4 %collective-permute-start = (bf16[2,256,1024]{2,1,0:T(8,128)(2,1)}, bf16[2,256,1024]{2,1,0:T(8,128)(2,1)}, u32[]{:S(2)}, u32[]{:S(2)}) collective-permute-start(bf16[2,256,1024]{2,1,0:T(8,128)(2,1)} %pad_maximum_fusion), channel_id=1, source_target_pairs={{0,16},{16,32},{32,48},{48,64},{64,80},{80,96},{96,112},{112,128},... | collective-permute-start | bytes 3145736 | tf_op jit(solution)/shard_map/ppermute | solution.py:17
  31.5 0.7 convolution_bitcast_fusion.1
  32.2 1.2 copy.69
  33.4 3.3 convolution_convert_fusion
  36.7 2.0 copy.67
  38.7 0.2 fusion.50
  38.9 1.1 copy_bitcast_fusion
  40.0 1.9 fusion.68
  41.9 0.4 subtract_convert_fusion.3
  42.3 10.3 %collective-permute-done = bf16[2,256,1024]{2,1,0:T(8,128)(2,1)} collective-permute-done((bf16[2,256,1024]{2,1,0:T(8,128)(2,1)}, bf16[2,256,1024]{2,1,0:T(8,128)(2,1)}, u32[]{:S(2)}, u32[]{:S(2)}) %collective-permute-start) | collective-permute-done | bytes 1048608 | tf_op jit(solution)/shard_map/ppermute | solution.py:17
  52.6 1.3 slice_bitcast_fusion.4
  53.9 0.1 copy.71
  54.0 0.1 copy.47
  54.1 0.1 copy.72
  54.2 0.1 copy.48
  54.3 0.6 copy-done.13
  54.9 0.8 fusion.42
  55.6 3.8 fusion.70
  59.5 2.7 fusion.32
  62.2 18.5 %fusion.28 = f32[256,8,128]{2,0,1:T(8,128)} fusion(f32[8,256,512]{2,1,0:T(8,128)} %fusion.32, bf16[256,8,128]{2,0,1:T(8,128)(2,1)} %copy-done.7, bf16[256,8,128]{2,0,1:T(8,128)(2,1)} %copy-done.13, f32[8,256,512]{2,1,0:T(8,128)} %get-tuple-element.42, f32[8,256]{1,0:T(8,128)S(1)} %get-tuple-element.41), kind=kOutput, calls=%fused_computation.24 | convolution fusion | flops 277875200 | bytes 10493952 | tf_op jit(solution)/shard_map/hqk,khd->qhd/dot_general | solution.py:86
  80.7 20.4 %fusion.19 = f32[512,8,128]{2,0,1:T(8,128)} fusion(f32[8,256,512]{2,1,0:T(8,128)} %fusion.32, bf16[256,8,64]{2,0,1:T(8,128)(2,1)} %copy-done.15, bf16[256,8,64]{2,0,1:T(8,128)(2,1)} %copy-done.14, f32[8,256,512]{2,1,0:T(8,128)} %get-tuple-element.42, f32[8,256]{1,0:T(8,128)S(1)} %get-tuple-element.41), kind=kOutput, calls=%fused_computation.19 | convolution fusion | flops 276826624 | bytes 11018240 | tf_op jit(solution)/shard_map/hqk,qhd->khd/dot_general | solution.py:89
  101.2 4.0 fusion.25
  105.3 2.4 subtract_convert_fusion.1
  107.6 1.1 pad_maximum_fusion.8
  108.7 2.1 copy.58
  110.8 3.6 fusion.72
  114.4 1.1 fusion.67
  115.5 1.1 pad_maximum_fusion.7
  116.6 2.1 copy.54
  118.7 2.3 pad_maximum_fusion.2
  121.0 1.3 collective-permute-start.1
  122.3 2.3 pad_maximum_fusion.6
  124.6 2.1 copy.53
  126.6 2.3 convolution_add_fusion.3
  129.0 0.8 convolution_add_fusion.2
  129.8 0.0 copy-start.22
  129.8 0.8 fusion.71
  130.5 16.8 %collective-permute-done.1 = bf16[2,256,1024]{1,2,0:T(8,128)(2,1)} collective-permute-done((bf16[2,256,1024]{1,2,0:T(8,128)(2,1)}, bf16[2,256,1024]{1,2,0:T(8,128)(2,1)}, u32[]{:S(2)}, u32[]{:S(2)}) %collective-permute-start.1) | collective-permute-done | bytes 1048608 | tf_op jit(solution)/shard_map/ppermute | solution.py:17
  147.3 1.8 fusion.43
  149.2 2.1 multiply_reduce_fusion.1
  151.2 2.1 fusion.36
  153.3 3.8 convolution_add_fusion
  157.1 0.0 all-reduce.6.cloned.1.call-update
  157.1 83.4 %all-reduce.1 = f32[1024]{0:T(1024)S(1)} all-reduce(f32[1024]{0:T(1024)S(1)} %get-tuple-element.4), channel_id=3, replica_groups=mesh['seq'=16,'dp'=16] {'seq','dp'}, use_global_device_ids=true, to_apply=%region_6.7.clone | all-reduce | flops 1024 | bytes 8192
  240.5 0.6 dynamic-slice.1
  241.1 192.3 %all-reduce.6.cloned.1.call-done = (f32[1024,1024]{1,0:T(8,128)}, f32[256,1024]{1,0:T(8,128)}) async-done(((f32[1024,1024]{1,0:T(8,128)}, f32[256,1024]{1,0:T(8,128)}), (f32[1024,1024]{1,0:T(8,128)}, f32[256,1024]{1,0:T(8,128)})) %all-reduce.6.cloned.1.call-update) | async-done | bytes 5242896
  433.4 1.4 constant_dynamic-slice_fusion.1
  434.8 1.4 constant_dynamic-slice_fusion
  (49 shorter events, 0.1 us)
Async XLA Ops:
  7.2 3.4 copy-start
  7.2 426.2 %all-reduce.6.cloned.1.call-start = ((), (), s32[]{:S(2)}) async-start(), calls=%async_computation | async-start | bytes 10485760
  9.7 0.8 copy-start.1
  17.1 0.8 copy-start.7
  21.2 10.3 %copy-start.2 = (bf16[256,1024]{1,0:T(8,128)(2,1)S(1)}, bf16[256,1024]{1,0:T(8,128)(2,1)}, u32[]{:S(2)}) copy-start(bf16[256,1024]{1,0:T(8,128)(2,1)} %copy-done.1) | copy-start | bytes 1572868
  21.2 10.3 %copy-start.4 = (bf16[1024,1024]{1,0:T(8,128)(2,1)S(1)}, bf16[1024,1024]{1,0:T(8,128)(2,1)}, u32[]{:S(2)}) copy-start(bf16[1024,1024]{1,0:T(8,128)(2,1)} %param.11) | copy-start | bytes 6291460
  23.8 8.4 %copy-start.17 = (bf16[256,1024]{1,0:T(8,128)(2,1)}, bf16[256,1024]{1,0:T(8,128)(2,1)S(1)}, u32[]{:S(2)}) copy-start(bf16[256,1024]{1,0:T(8,128)(2,1)S(1)} %convolution_convert_fusion.1) | copy-start | bytes 1572868
  26.1 26.5 %collective-permute-start = (bf16[2,256,1024]{2,1,0:T(8,128)(2,1)}, bf16[2,256,1024]{2,1,0:T(8,128)(2,1)}, u32[]{:S(2)}, u32[]{:S(2)}) collective-permute-start(bf16[2,256,1024]{2,1,0:T(8,128)(2,1)} %pad_maximum_fusion), channel_id=1, source_target_pairs={{0,16},{16,32},{32,48},{48,64},{64,80},{80,96},{96,112},{112,128},... | collective-permute-start | bytes 3145736 | tf_op jit(solution)/shard_map/ppermute | solution.py:17
  41.9 13.0 %copy-start.8 = (bf16[256,8,128]{2,0,1:T(8,128)(2,1)S(1)}, bf16[256,8,128]{2,0,1:T(8,128)(2,1)}, u32[]{:S(2)}) copy-start(bf16[256,8,128]{2,0,1:T(8,128)(2,1)} %copy-done.7) | copy-start | bytes 1572868
  42.3 11.9 %copy-start.14 = (bf16[256,8,64]{2,0,1:T(8,128)(2,1)}, bf16[256,8,64]{2,0,1:T(8,128)(2,1)S(1)}, u32[]{:S(2)}) copy-start(bf16[256,8,64]{2,0,1:T(8,128)(2,1)S(1)} %get-tuple-element.11) | copy-start | bytes 786436
  42.3 11.9 %copy-start.15 = (bf16[256,8,64]{2,0,1:T(8,128)(2,1)}, bf16[256,8,64]{2,0,1:T(8,128)(2,1)S(1)}, u32[]{:S(2)}) copy-start(bf16[256,8,64]{2,0,1:T(8,128)(2,1)S(1)} %get-tuple-element.12) | copy-start | bytes 786436
  54.1 0.8 copy-start.13
  55.6 3.8 copy-start.18
  101.2 4.0 copy-start.6
  101.2 4.0 copy-start.10
  101.2 4.0 copy-start.20
  101.2 4.0 copy-start.21
  110.8 3.6 copy-start.19
  110.8 4.7 %copy-start.11 = (bf16[256,8,64]{2,0,1:T(8,128)(2,1)S(1)}, bf16[256,8,64]{2,0,1:T(8,128)(2,1)}, u32[]{:S(2)}) copy-start(bf16[256,8,64]{2,0,1:T(8,128)(2,1)} %get-tuple-element.7) | copy-start | bytes 786436
  110.8 4.7 %copy-start.12 = (bf16[256,8,64]{2,0,1:T(8,128)(2,1)S(1)}, bf16[256,8,64]{2,0,1:T(8,128)(2,1)}, u32[]{:S(2)}) copy-start(bf16[256,8,64]{2,0,1:T(8,128)(2,1)} %get-tuple-element.8) | copy-start | bytes 786436
  121.0 26.4 %collective-permute-start.1 = (bf16[2,256,1024]{1,2,0:T(8,128)(2,1)}, bf16[2,256,1024]{1,2,0:T(8,128)(2,1)}, u32[]{:S(2)}, u32[]{:S(2)}) collective-permute-start(bf16[2,256,1024]{1,2,0:T(8,128)(2,1)} %pad_maximum_fusion.2), channel_id=1, source_target_pairs={{16,0},{32,16},{48,32},{64,48},{80,64},{96,80},{112,96},{128,112},... | collective-permute-start | bytes 3145736 | tf_op jit(solution)/shard_map/ppermute | solution.py:17
  126.6 2.3 copy-start.5
  126.6 2.3 copy-start.16
  126.6 3.1 copy-start.3
  126.6 3.1 copy-start.9
  129.8 19.4 %copy-start.22 = (f32[1024]{0:T(1024)S(1)}, f32[1024]{0:T(1024)}, u32[]{:S(2)}) copy-start(f32[1024]{0:T(1024)} %param.10) | copy-start | bytes 12292
  149.1 2.1 copy-start.23
Sparse Core Ops, SparseCore 0:
  157.2 276.1 all-reduce.5
where the time goes:
time: 445 us; the launch traced here: 443 us
  waiting for transfers between devices  219 us (49%)
  blocking collectives  83.4 us (19%)
  matrix products  72.6 us (16%)
  local copies, waits for them, and re-layouts  25.8 us (6%)
  other arithmetic  20.8 us (5%)
  between operations  14.4 us (3%)
  starting transfers between devices  6.69 us (2%)
    unnamed x2, waiting for transfers between devices  192 us
    unnamed x1, blocking collectives  83.4 us
    ppermute x2, waiting for transfers between devices, shifted(): lax.ppermute(value, axis, [(source, source + steps) for source in range(i...  27 us
    dot_general x1, matrix products, band_attention(): jnp.einsum('hqk,qhd->khd', grad_scores, query_h, preferred_element_type=j...  20.4 us
    dot_general x1, matrix products, band_attention(): jnp.einsum('hqk,khd->qhd', grad_scores, key_h, preferred_element_type=jnp...  18.5 us
    dot_general x5, matrix products, against(): lax.dot_general(left_op, right_op, (((1,), (1,)), ((), ())), preferred_el...  10.6 us
    dot_general x5, matrix products, product(): return jnp.dot(left_op, right_op, preferred_element_type=jnp.float32)  8.92 us
  transfers between devices with their start and end apart: 3, of which 3 were waited for; matrix products, arithmetic and copies ran while one was open for 4% of the time, Pallas kernels for 0%

commit v1 on v0

v1 whole, which is shorter than its diff:
```python
import math

import jax
import jax.numpy as jnp
import numpy as np
from jax import lax
from jax.experimental import pallas as pl
from jax.experimental.pallas import tpu as pltpu
from jax.sharding import PartitionSpec as P

HEADS = 8
HEAD_DIM = 128
D = 1024
VOCAB = 256
TOK = 256
N_Z = 8
N_DP = 16
MEMBERS = 32
NEGATIVE = -1e30
EPSILON = 1e-05
THETA = 10000.0
AXES = ("seq", "dp")
BF = jnp.bfloat16
F32 = jnp.float32
VMEM_LIMIT = 56 * 1024 * 1024


def plane_groups():
    return [[(y * N_Z + z) * N_DP + d for y in range(2) for d in range(N_DP)] for z in range(N_Z)]


def ring_groups():
    return [[(y * N_Z + z) * N_DP + d for z in range(N_Z)] for y in range(2) for d in range(N_DP)]


def exchange(value, groups):
    return lax.all_to_all(value, AXES, 0, 0, axis_index_groups=groups, tiled=False)


def angle_tables():
    inverse = THETA ** (-np.arange(HEAD_DIM // 2, dtype=np.float64) / (HEAD_DIM // 2))
    near = np.arange(-TOK, TOK, dtype=np.float64)[:, None] * inverse[None, :]
    base = (TOK * np.arange(16, dtype=np.float64))[:, None] * inverse[None, :]

    def wide(angle):
        cosine, sine = np.cos(angle), np.sin(angle)
        return np.stack(
            [np.concatenate([cosine, cosine], -1), np.concatenate([-sine, sine], -1)]
        ).astype(np.float32)

    return wide(near), wide(base)


def mm(left, right):
    return lax.dot_general(left, right, (((1,), (0,)), ((), ())), preferred_element_type=F32)


def mm_nt(left, right):
    return lax.dot_general(left, right, (((1,), (1,)), ((), ())), preferred_element_type=F32)


def mm_tn(left, right):
    return lax.dot_general(left, right, (((0,), (0,)), ((), ())), preferred_element_type=F32)


def table_row(ids):
    return (ids & 128) | ((ids & 15) << 3) | ((ids >> 4) & 7)


def hot_columns(ids_row):
    place = lax.broadcasted_iota(jnp.int32, (VOCAB, TOK), 0)
    return (place == table_row(ids_row)).astype(F32).astype(BF)


def turn_tables(near_ref, base_ref, rows, block):
    near_c, near_s = near_ref[0, rows, :], near_ref[1, rows, :]
    base_c, base_s = base_ref[0, pl.ds(block, 1), :], base_ref[1, pl.ds(block, 1), :]
    return near_c * base_c - near_s * base_s, near_s * base_c + near_c * base_s


def turn(value, cosine, sine):
    return value * cosine + pltpu.roll(value, HEAD_DIM // 2, 1) * sine


def turn_back(value, cosine, sine):
    return value * cosine - pltpu.roll(value, HEAD_DIM // 2, 1) * sine


def head(index):
    return slice(index * HEAD_DIM, (index + 1) * HEAD_DIM)


def project_kernel(
    ids_ref, gain_ref, near_ref, base_ref, emb_any, wk_any, wv_any, wq_any, do_any, wo_any,
    q_ref, k_ref, v_ref, ga_ref, ktab_ref, vtab_ref,
    emb, wk, wv, wq, do, wo, qtab, sems,
):
    pairs = [(emb_any, emb), (wk_any, wk), (wv_any, wv), (wq_any, wq), (do_any, do), (wo_any, wo)]
    copies = [pltpu.make_async_copy(s, d, sems.at[i]) for i, (s, d) in enumerate(pairs)]
    for copy in copies:
        copy.start()
    block = lax.axis_index("seq")
    hot = hot_columns(ids_ref[...])
    cosine, sine = turn_tables(near_ref, base_ref, slice(TOK, 2 * TOK), block)
    order = lax.broadcasted_iota(jnp.int32, (VOCAB, VOCAB), 0)
    value = (order & 128) | ((order & 7) << 4) | ((order >> 3) & 15)
    swap = (lax.broadcasted_iota(jnp.int32, (VOCAB, VOCAB), 1) == value).astype(F32).astype(BF)
    copies[0].wait()
    inputs = mm(swap, emb[...])
    recip = lax.rsqrt(jnp.mean(inputs * inputs, axis=-1, keepdims=True) + EPSILON)
    normed = (inputs * recip * gain_ref[...]).astype(BF)
    hot2 = jnp.concatenate([hot, hot], axis=0)

    def fill(tab_ref, weight):
        full = mm(normed, weight[...])
        high = full.astype(BF)
        tab_ref[:VOCAB, :] = high
        tab_ref[VOCAB:, :] = (full - high.astype(F32)).astype(BF)

    def gather(tab_ref, out_ref):
        full = mm_tn(hot2, tab_ref[...])
        for h in range(HEADS):
            out_ref[:, head(h)] = turn(full[:, head(h)], cosine, sine).astype(BF)

    copies[1].wait()
    fill(ktab_ref, wk)
    gather(ktab_ref, k_ref)
    copies[2].wait()
    vtab_ref[...] = mm(normed, wv[...]).astype(BF)
    v_ref[...] = mm_tn(hot, vtab_ref[...]).astype(BF)
    copies[3].wait()
    fill(qtab, wq)
    gather(qtab, q_ref)
    copies[4].wait()
    copies[5].wait()
    ga_ref[...] = mm(do[...], wo[...]).astype(BF)


def attend_kernel(
    ids_ref, prev_ref, near_ref, base_ref, q_ref, k_ref, v_ref, ga_ref, ktab_ref, vtab_ref,
    wq_any, wk_any, wv_any,
    out_ref,
    kprev, vprev, gq, kg, vg, wq, wk, wv, sems,
):
    pairs = [(wq_any, wq), (wk_any, wk), (wv_any, wv)]
    copies = [pltpu.make_async_copy(s, d, sems.at[i]) for i, (s, d) in enumerate(pairs)]
    for copy in copies:
        copy.start()
    block = lax.axis_index("seq")
    lead = jnp.where(block == 0, NEGATIVE, 0.0).astype(F32)
    hot_own = hot_columns(ids_ref[...])
    hot_prev = hot_columns(prev_ref[...])
    cos_p, sin_p = turn_tables(near_ref, base_ref, slice(0, TOK), block)
    cos_o, sin_o = turn_tables(near_ref, base_ref, slice(TOK, 2 * TOK), block)
    full = mm_tn(jnp.concatenate([hot_prev, hot_prev], axis=0), ktab_ref[...])
    for h in range(HEADS):
        kprev[:, head(h)] = turn(full[:, head(h)], cos_p, sin_p).astype(BF)
    vprev[...] = mm_tn(hot_prev, vtab_ref[...]).astype(BF)
    scale = HEAD_DIM ** (-0.5)
    own = lax.broadcasted_iota(jnp.int32, (TOK, TOK), 0) <= lax.broadcasted_iota(
        jnp.int32, (TOK, TOK), 1
    )
    for h in range(HEADS):
        query, grad = q_ref[:, head(h)], ga_ref[:, head(h)]
        key_o, key_p = k_ref[:, head(h)], kprev[:, head(h)]
        value_o, value_p = v_ref[:, head(h)], vprev[:, head(h)]
        scores = jnp.where(own, mm_nt(key_o, query), mm_nt(key_p, query) + lead)
        highest = jnp.max(scores, axis=0, keepdims=True)
        weights = jnp.exp((scores - highest) * scale)
        probs = weights * (1.0 / jnp.sum(weights, axis=0, keepdims=True))
        grad_probs = jnp.where(own, mm_nt(value_o, grad), mm_nt(value_p, grad))
        delta = jnp.sum(probs * grad_probs, axis=0, keepdims=True)
        grad_scores = probs * (grad_probs - delta) * scale
        probs_o = jnp.where(own, probs, 0.0).astype(BF)
        probs_p = jnp.where(own, 0.0, probs).astype(BF)
        gs_o = jnp.where(own, grad_scores, 0.0).astype(BF)
        gs_p = jnp.where(own, 0.0, grad_scores).astype(BF)
        vg[:TOK, head(h)] = mm(probs_p, grad).astype(BF)
        vg[TOK:, head(h)] = mm(probs_o, grad).astype(BF)
        kg[:TOK, head(h)] = turn_back(mm(gs_p, query), cos_p, sin_p).astype(BF)
        kg[TOK:, head(h)] = turn_back(mm(gs_o, query), cos_o, sin_o).astype(BF)
        grad_q = mm_tn(gs_o, key_o) + mm_tn(gs_p, key_p)
        gq[:, head(h)] = turn_back(grad_q, cos_o, sin_o).astype(BF)
    hot2 = jnp.concatenate([hot_prev, hot_own], axis=1)
    key_table = mm(hot2, kg[...]).astype(BF)
    out_ref[:, :D] = key_table
    value_table = mm(hot2, vg[...]).astype(BF)
    query_table = mm(hot_own, gq[...]).astype(BF)
    for copy in copies:
        copy.wait()
    grad_normed = mm_nt(query_table, wq[...]) + mm_nt(key_table, wk[...]) + mm_nt(value_table, wv[...])
    out_ref[:, D:] = grad_normed.astype(BF)


def rows_kernel(emb_ref, gain_ref, scaled_ref, pick_ref, row_ref, spread):
    block, lane = lax.axis_index("seq"), lax.axis_index("dp")
    high, ring = block // N_Z, lax.rem(block, N_Z)
    first = high * 128 + lane
    rows = lax.broadcasted_iota(jnp.int32, (8, VOCAB), 0) * 16 + first
    hot = (lax.broadcasted_iota(jnp.int32, (8, VOCAB), 1) == rows).astype(F32).astype(BF)
    inputs = mm(hot, emb_ref[...])
    recip = lax.rsqrt(jnp.mean(inputs * inputs, axis=-1, keepdims=True) + EPSILON)
    scaled = inputs * recip
    scaled_ref[...] = scaled
    normed = (scaled * gain_ref[...]).astype(BF)
    place = lax.broadcasted_iota(jnp.int32, (D, 256), 1)
    member = place >> 3
    column = ((member >> 4) << 9) + ring * 64 + ((member & 15) << 2) + (place & 3)
    choose = (lax.broadcasted_iota(jnp.int32, (D, 256), 0) == column).astype(F32).astype(BF)
    picked = mm(normed, choose)
    pick_ref[...] = jnp.concatenate([picked, picked], axis=0).astype(BF)
    for k in range(8):
        spread[:, k, :] = inputs[:, k * 128 : (k + 1) * 128]
    row_ref[...] = spread[ring]


def ring_kernel(got_ref, scaled_ref, out_ref, spread, terms):
    total = jnp.sum(got_ref[...].astype(F32), axis=0)
    key_part, grad_part = total[:, :D], total[:, D:]
    product = jnp.sum(grad_part * scaled_ref[...], axis=0, keepdims=True)
    for k in range(8):
        spread[:, k, :] = grad_part[:, k * 128 : (k + 1) * 128]
        terms[k : k + 1, :] = product[:, k * 128 : (k + 1) * 128]
    out_ref[:, :, :D] = jnp.broadcast_to(key_part.astype(BF)[None], (N_Z, 8, D))
    out_ref[:, :, D : D + 128] = spread[...].astype(BF)
    out_ref[:, :, D + 128 :] = jnp.broadcast_to(terms[...].astype(BF)[None], (N_Z, 8, 128))


def weight_kernel(got_ref, pick_ref, row_ref, gain_ref, out_ref, ge_ref):
    total = jnp.sum(got_ref[...].astype(F32), axis=0)
    keys = total[:, :D]
    high = keys.astype(BF).astype(F32)
    both = jnp.concatenate([high, keys - high], axis=0).astype(BF)
    part = mm_tn(pick_ref[...], both)
    first = (lax.broadcasted_iota(jnp.int32, (256, 512), 0) & 4) == 0
    part = jnp.where(first, part[:, :512], part[:, 512:])
    out_ref[:, :, :512] = part.reshape(MEMBERS, 8, 512).astype(BF)
    out_ref[:, :, 512:] = jnp.broadcast_to(total[:, D + 128 :].astype(BF)[None], (MEMBERS, 8, 128))
    grad_normed = total[:, D : D + 128]
    inputs = row_ref[...]

    def mean(value):
        return jnp.sum(jnp.sum(value, axis=1, keepdims=True), axis=0, keepdims=True) * (1.0 / D)

    recip = lax.rsqrt(mean(inputs * inputs) + EPSILON)
    grad_scaled = grad_normed * gain_ref[...]
    ge_ref[...] = recip * grad_scaled - inputs * (recip * recip * recip) * mean(grad_scaled * inputs)


def finish_kernel(got_ref, gk_ref, gg_ref):
    total = jnp.sum(got_ref[...].astype(F32), axis=0)
    gk_ref[:, :512] = total[:4, :512]
    gk_ref[:, 512:] = total[4:, :512]
    gg_ref[...] = total[:, 512:]


def call(kernel, outs, ins, scratch=(), flops=0, moved=0):
    any_space = pl.BlockSpec(memory_space=pl.ANY)
    vmem = pl.BlockSpec(memory_space=pltpu.VMEM)
    return pl.pallas_call(
        kernel,
        out_shape=[jax.ShapeDtypeStruct(shape, kind) for shape, kind in outs],
        in_specs=[any_space if far else vmem for _, far in ins],
        out_specs=[vmem] * len(outs),
        scratch_shapes=list(scratch),
        compiler_params=pltpu.CompilerParams(vmem_limit_bytes=VMEM_LIMIT),
        cost_estimate=pl.CostEstimate(flops=flops, bytes_accessed=moved, transcendentals=0),
    )(*[value for value, _ in ins])


def local(byte_ids, embedding, gain, w_query, w_key, w_value, w_out, d_output):
    near_table, base_table = (jnp.asarray(table) for table in angle_tables())
    block, lane = lax.axis_index("seq"), lax.axis_index("dp")
    prev_ids = lax.ppermute(byte_ids, "seq", [(i, i + 1) for i in range(15)])
    gain_row = gain.reshape(1, D)
    gain_tile = gain.reshape(8, 128)
    wide = ((TOK, D), BF)
    mat = pltpu.VMEM((D, D), BF)
    tall = pltpu.VMEM((2 * TOK, D), BF)
    flat = pltpu.VMEM((TOK, D), BF)
    near = lambda *values: [(value, False) for value in values]
    far = lambda *values: [(value, True) for value in values]
    q, k, v, ga, ktab, vtab = call(
        project_kernel,
        [wide, wide, wide, wide, ((2 * VOCAB, D), BF), wide],
        near(byte_ids, gain_row, near_table, base_table)
        + far(embedding, w_key, w_value, w_query, d_output[0], w_out),
        [flat, mat, mat, mat, flat, mat, tall, pltpu.SemaphoreType.DMA((6,))],
        flops=4_000_000_000,
        moved=14_000_000,
    )
    (tables,) = call(
        attend_kernel,
        [((VOCAB, 2 * D), BF)],
        near(byte_ids, prev_ids, near_table, base_table, q, k, v, ga, ktab, vtab)
        + far(w_query, w_key, w_value),
        [flat, flat, flat, tall, tall, mat, mat, mat, pltpu.SemaphoreType.DMA((3,))],
        flops=5_000_000_000,
        moved=12_000_000,
    )
    first = exchange(tables.reshape(MEMBERS, 8, 2 * D), plane_groups())
    embedding_later, _ = lax.optimization_barrier((embedding, tables))
    scaled, pick, row = call(
        rows_kernel,
        [((8, D), F32), ((16, 256), BF), ((8, 128), F32)],
        near(embedding_later, gain_row),
        [pltpu.VMEM((8, 8, 128), F32)],
        flops=10_000_000,
        moved=600_000,
    )
    (ring,) = call(
        ring_kernel,
        [((N_Z, 8, D + 256), BF)],
        near(first, scaled),
        [pltpu.VMEM((8, 8, 128), F32), pltpu.VMEM((8, 128), F32)],
        flops=1_000_000,
        moved=1_000_000,
    )
    second = exchange(ring, ring_groups())
    part, grad_row = call(
        weight_kernel,
        [((MEMBERS, 8, 640), BF), ((8, 128), F32)],
        near(second, pick, row, gain_tile),
        flops=10_000_000,
        moved=400_000,
    )
    third = exchange(part, plane_groups())
    gk, gg = call(
        finish_kernel,
        [((4, D), F32), ((8, 128), F32)],
        near(third),
        flops=1_000_000,
        moved=400_000,
    )
    gg_own = lax.dynamic_slice(gg.reshape(D), ((block * N_DP + lane) * 4,), (4,))
    return gk, gg_own, grad_row.reshape(1, D)


def solution(mesh):
    in_specs = (P("dp", "seq"), P(), P(), P(), P(), P(), P(), P("dp", "seq", None))
    out_specs = (P(("seq", "dp"), None), P(("seq", "dp")), P(("seq", "dp"), None))
    return jax.shard_map(local, mesh=mesh, in_specs=in_specs, out_specs=out_specs, check_vma=False)
```

time: 445 us -> 89.9 us (0.20)
  waiting for transfers between devices: 219 us -> 24.5 us
  matrix products: 72.6 us -> 0 us
  blocking collectives: 83.4 us -> 16 us
  Pallas kernels: 0 us -> 26.4 us
  local copies, waits for them, and re-layouts: 25.8 us -> 3.52 us
  other arithmetic: 20.8 us -> 0 us
  between operations: 14.4 us -> 0.7 us
  starting transfers between devices: 6.69 us -> 18.2 us
    unnamed x2 -> x0, waiting for transfers between devices: 192 us -> none
    unnamed x1 -> x0, blocking collectives: 83.4 us -> none
    dot_general x18 -> x0, matrix products: 72.6 us -> none  [the longest x1 20.4 us: band_attention(): jnp.einsum('hqk,qhd->khd', grad_scores, query_h, preferred_element_type=j...]
    ppermute x2 -> x1, waiting for transfers between devices: 27 us -> 0.01 us  [local(): prev_ids = lax.ppermute(byte_ids, 'seq', [(i, i + 1) for i in range(15)])]
    pallas_call x0 -> x6, Pallas kernels: none -> 26.4 us  [call(): pl.pallas_call(kernel, out_shape=[jax.ShapeDtypeStruct(shape, kind) for s...]
    all_to_all x0 -> x2, waiting for transfers between devices: none -> 24.5 us  [exchange(): lax.all_to_all(value, AXES, 0, 0, axis_index_groups=groups, tiled=False)]
    all_to_all x0 -> x1, blocking collectives: none -> 16 us  [exchange(): lax.all_to_all(value, AXES, 0, 0, axis_index_groups=groups, tiled=False)]
    all_to_all x0 -> x2, starting transfers between devices: none -> 13.8 us  [exchange(): lax.all_to_all(value, AXES, 0, 0, axis_index_groups=groups, tiled=False)]
  transfers between devices with their start and end apart: 3 -> 3, of which waited for: 3 -> 2; matrix products, arithmetic and copies ran while one was open for 4% -> 0% of each run, Pallas kernels for 0% -> 11%
where the time goes in v1:
time: 89.9 us; the launch traced here: 89.3 us
  Pallas kernels  26.4 us (29%)
  waiting for transfers between devices  24.5 us (27%)
  starting transfers between devices  18.2 us (20%)
  blocking collectives  16 us (18%)
  local copies, waits for them, and re-layouts  3.52 us (4%)
    pallas_call x6, Pallas kernels, call(): pl.pallas_call(kernel, out_shape=[jax.ShapeDtypeStruct(shape, kind) for s...  26.4 us
    all_to_all x2, waiting for transfers between devices, exchange(): lax.all_to_all(value, AXES, 0, 0, axis_index_groups=groups, tiled=False)  24.5 us
    all_to_all x1, blocking collectives, exchange(): lax.all_to_all(value, AXES, 0, 0, axis_index_groups=groups, tiled=False)  16 us
    all_to_all x2, starting transfers between devices, exchange(): lax.all_to_all(value, AXES, 0, 0, axis_index_groups=groups, tiled=False)  13.8 us
    ppermute x1, starting transfers between devices, local(): prev_ids = lax.ppermute(byte_ids, 'seq', [(i, i + 1) for i in range(15)])  4.37 us
    unnamed x6, local copies, waits for them, and re-layouts  2.25 us
  transfers between devices with their start and end apart: 3, of which 2 were waited for; matrix products, arithmetic and copies ran while one was open for 0% of the time, Pallas kernels for 11%

profile of v1, /device:TPU:1, one launch (start us, length us, event | category | flops | bytes accessed | tf_op | source)
XLA Modules:
  0.0 89.3 jit_solution(10827961140295995292)
XLA Ops:
  0.6 4.4 %collective-permute-start = (s32[1,256]{1,0:T(1,128)}, s32[1,256]{1,0:T(1,128)S(1)}, u32[]{:S(2)}, u32[]{:S(2)}) collective-permute-start(s32[1,256]{1,0:T(1,128)} %ids_ref.3), channel_id=1, source_target_pairs={{0,16},{16,32},{32,48},{48,64},{64,80},{80,96},{96,112},{112,128},... | collective-permute-start | bytes 3080 | tf_op jit(solution)/shard_map/ppermute | solution.py:274
  5.0 7.9 %shard_map.121 = (bf16[256,1024]{1,0:T(8,128)(2,1)}, bf16[256,1024]{1,0:T(8,128)(2,1)}, bf16[256,1024]{1,0:T(8,128)(2,1)}, bf16[256,1024]{1,0:T(8,128)(2,1)}, bf...) custom-call(s32[1,256]{1,0:T(1,128)} %ids_ref.3, f32[1,1024]{1,0:T(1,128)} %bitcast.7, ...), custom_call_target="tpu_custom_call" | custom-call | flops 4000000000 | bytes 14000000 | tf_op jit(solution)/shard_map/pallas_call | solution.py:260
  13.0 0.0 collective-permute-done.prev_ref
  13.0 0.0 copy-start.2
  13.0 0.6 copy-done.2
  13.5 10.6 %shard_map.122 = bf16[256,2048]{1,0:T(8,128)(2,1)} custom-call(s32[1,256]{1,0:T(1,128)} %ids_ref.3, s32[1,256]{1,0:T(1,128)} %copy-done.2, f32[2,512,128]{2,1,0:T(8,128)} %constant.19.clone.near_ref, f32[2,16,128]{2,1,0:T(8,128)} %constant.20.clone.base_ref, bf16[256,1024]{1,0:T(8,128)(2,1)} %get-tuple-element.17.q_ref, ...), custom_call_target="tpu_custom_call" | custom-call | flops 5000000000 | bytes 12000000 | tf_op jit(solution)/shard_map/pallas_call | solution.py:260
  24.1 8.1 %all-to-all-start = ((bf16[32,8,2048]{2,1,0:T(8,128)(2,1)}), bf16[32,8,2048]{2,1,0:T(8,128)(2,1)S(1)}, u32[]{:S(2)}, u32[]{:S(2)}) async-start(bf16[32,8,2048]{2,1,0:T(8,128)(2,1)} %bitcast.6), calls=%async_computation | async-start | bytes 2097152 | tf_op jit(solution)/shard_map/all_to_all | solution.py:37
  32.2 2.2 %shard_map.123 = (f32[8,1024]{1,0:T(8,128)}, bf16[16,256]{1,0:T(8,128)(2,1)}, f32[8,128]{1,0:T(8,128)}) custom-call(bf16[256,1024]{1,0:T(8,128)(2,1)} %emb_ref, f32[1,1024]{1,0:T(1,128)} %bitcast.8), custom_call_target="tpu_custom_call" | custom-call | flops 10000000 | bytes 600000 | tf_op jit(solution)/shard_map/pallas_call | solution.py:260
  34.4 15.0 %all-to-all-done.got_ref = bf16[32,8,2048]{2,1,0:T(8,128)(2,1)S(1)} async-done(((bf16[32,8,2048]{2,1,0:T(8,128)(2,1)}), bf16[32,8,2048]{2,1,0:T(8,128)(2,1)S(1)}, u32[]{:S(2)}, u32[]{:S(2)}) %all-to-all-start) | async-done | bytes 1048608 | tf_op jit(solution)/shard_map/all_to_all | solution.py:37
  49.3 0.0 copy-start
  49.4 1.0 %copy-done = bf16[32,8,2048]{2,1,0:T(8,128)(2,1)} copy-done((bf16[32,8,2048]{2,1,0:T(8,128)(2,1)}, bf16[32,8,2048]{2,1,0:T(8,128)(2,1)S(1)}, u32[]{:S(2)}) %copy-start) | copy-done | bytes 1048600
  50.3 2.1 %shard_map.124 = bf16[8,8,1280]{2,1,0:T(8,128)(2,1)} custom-call(bf16[32,8,2048]{2,1,0:T(8,128)(2,1)} %copy-done, f32[8,1024]{1,0:T(8,128)} %get-tuple-element.24.scaled_ref), custom_call_target="tpu_custom_call" | custom-call | flops 1000000 | bytes 1000000 | tf_op jit(solution)/shard_map/pallas_call | solution.py:260
  52.4 16.0 %all_to_all.15.got_ref = bf16[8,8,1280]{2,1,0:T(8,128)(2,1)} all-to-all(bf16[8,8,1280]{2,1,0:T(8,128)(2,1)} %shard_map.124), channel_id=1, replica_groups={{0,16,32,48,64,80,96,112},{1,17,33,49,65,81,97,113},{2,18,34,50,66,82,9..., dimensions={0} | all-to-all | bytes 327680 | tf_op jit(solution)/shard_map/all_to_all | solution.py:37
  68.4 2.0 %shard_map.125 = (bf16[32,8,640]{2,1,0:T(8,128)(2,1)}, f32[8,128]{1,0:T(8,128)}) custom-call(bf16[8,8,1280]{2,1,0:T(8,128)(2,1)} %all_to_all.15.got_ref, bf16[16,256]{1,0:T(8,128)(2,1)} %get-tuple-element.25.pick_ref, f32[8,128]{1,0:T(8,128)} %get-tuple-element.26.row_ref, f32[8,128]{1,0:T(8,128)} %bitcast.9), custom_call_target="tpu_custom_call" | custom-call | flops 10000000 | bytes 400000 | tf_op jit(solution)/shard_map/pallas_call | solution.py:260
  70.4 5.8 %all-to-all-start.2 = ((bf16[32,8,640]{2,1,0:T(8,128)(2,1)}), bf16[32,8,640]{2,1,0:T(8,128)(2,1)S(1)}, u32[]{:S(2)}, u32[]{:S(2)}) async-start(bf16[32,8,640]{2,1,0:T(8,128)(2,1)} %get-tuple-element.27), calls=%async_computation.2 | async-start | bytes 655360 | tf_op jit(solution)/shard_map/all_to_all | solution.py:37
  76.1 9.6 %all-to-all-done.2.got_ref = bf16[32,8,640]{2,1,0:T(8,128)(2,1)S(1)} async-done(((bf16[32,8,640]{2,1,0:T(8,128)(2,1)}), bf16[32,8,640]{2,1,0:T(8,128)(2,1)S(1)}, u32[]{:S(2)}, u32[]{:S(2)}) %all-to-all-start.2) | async-done | bytes 327712 | tf_op jit(solution)/shard_map/all_to_all | solution.py:37
  85.7 0.0 copy-start.1
  85.7 0.7 copy-done.1
  86.4 1.6 %shard_map.126 = (f32[4,1024]{1,0:T(4,128)}, f32[8,128]{1,0:T(8,128)}) custom-call(bf16[32,8,640]{2,1,0:T(8,128)(2,1)} %copy-done.1), custom_call_target="tpu_custom_call" | custom-call | flops 1000000 | bytes 400000 | tf_op jit(solution)/shard_map/pallas_call | solution.py:260
  88.1 1.3 %dynamic_slice.3 = f32[4]{0:T(128)} dynamic-slice(f32[1024]{0:T(1024)} %bitcast.12, s32[]{:T(128)S(6)} %select_n.3), dynamic_slice_sizes={4} | dynamic-slice | bytes 36 | tf_op jit(solution)/shard_map/dynamic_slice | solution.py:335
Async XLA Ops:
  0.6 12.3 %collective-permute-start = (s32[1,256]{1,0:T(1,128)}, s32[1,256]{1,0:T(1,128)S(1)}, u32[]{:S(2)}, u32[]{:S(2)}) collective-permute-start(s32[1,256]{1,0:T(1,128)} %ids_ref.3), channel_id=1, source_target_pairs={{0,16},{16,32},{32,48},{48,64},{64,80},{80,96},{96,112},{112,128},... | collective-permute-start | bytes 3080 | tf_op jit(solution)/shard_map/ppermute | solution.py:274
  13.0 0.6 copy-start.2
  24.1 25.2 %all-to-all-start = ((bf16[32,8,2048]{2,1,0:T(8,128)(2,1)}), bf16[32,8,2048]{2,1,0:T(8,128)(2,1)S(1)}, u32[]{:S(2)}, u32[]{:S(2)}) async-start(bf16[32,8,2048]{2,1,0:T(8,128)(2,1)} %bitcast.6), calls=%async_computation | async-start | bytes 2097152 | tf_op jit(solution)/shard_map/all_to_all | solution.py:37
  49.3 1.0 %copy-start = (bf16[32,8,2048]{2,1,0:T(8,128)(2,1)}, bf16[32,8,2048]{2,1,0:T(8,128)(2,1)S(1)}, u32[]{:S(2)}) copy-start(bf16[32,8,2048]{2,1,0:T(8,128)(2,1)S(1)} %all-to-all-done.got_ref) | copy-start | bytes 3145732
  70.4 15.3 %all-to-all-start.2 = ((bf16[32,8,640]{2,1,0:T(8,128)(2,1)}), bf16[32,8,640]{2,1,0:T(8,128)(2,1)S(1)}, u32[]{:S(2)}, u32[]{:S(2)}) async-start(bf16[32,8,640]{2,1,0:T(8,128)(2,1)} %get-tuple-element.27), calls=%async_computation.2 | async-start | bytes 655360 | tf_op jit(solution)/shard_map/all_to_all | solution.py:37
  85.7 0.7 copy-start.1

commit v2 on v1

v2 whole, which is shorter than its diff:
```python
import jax
import jax.numpy as jnp
import numpy as np
from jax import lax
from jax.experimental import pallas as pl
from jax.experimental.pallas import tpu as pltpu
from jax.sharding import PartitionSpec as P

HEADS = 8
HEAD_DIM = 128
D = 1024
VOCAB = 256
TOK = 256
N = 16
NEGATIVE = -1e30
EPSILON = 1e-05
THETA = 10000.0
BF = jnp.bfloat16
F32 = jnp.float32
MIB = 1024 * 1024

PLANE = 32
RING = 8
WIDE = 2 * D + 256
ROUNDS = ((1,), (2,), (4,))


def exchange(value):
    groups = [[(y * RING + z) * N + d for y in range(2) for d in range(N)] for z in range(RING)]
    return lax.all_to_all(value, ("seq", "dp"), 0, 0, axis_index_groups=groups, tiled=False)


def swap(value, step):
    return lax.ppermute(value, "seq", [(i, i ^ step) for i in range(N)])


def angle_tables():
    inverse = THETA ** (-np.arange(HEAD_DIM // 2, dtype=np.float64) / (HEAD_DIM // 2))
    near = np.arange(-TOK, TOK, dtype=np.float64)[:, None] * inverse[None, :]
    base = (TOK * np.arange(16, dtype=np.float64))[:, None] * inverse[None, :]

    def wide(angle):
        cosine, sine = np.cos(angle), np.sin(angle)
        return np.stack(
            [np.concatenate([cosine, cosine], -1), np.concatenate([-sine, sine], -1)]
        ).astype(np.float32)

    return wide(near), wide(base)


def mm(left, right):
    return lax.dot_general(left, right, (((1,), (0,)), ((), ())), preferred_element_type=F32)


def mm_nt(left, right):
    return lax.dot_general(left, right, (((1,), (1,)), ((), ())), preferred_element_type=F32)


def mm_tn(left, right):
    return lax.dot_general(left, right, (((0,), (0,)), ((), ())), preferred_element_type=F32)


def table_row(ids):
    return (ids & 128) | ((ids & 15) << 3) | ((ids >> 4) & 7)


def hot_columns(ids_row):
    place = lax.broadcasted_iota(jnp.int32, (VOCAB, TOK), 0)
    return (place == table_row(ids_row)).astype(F32).astype(BF)


def turn_tables(near_ref, base_ref, rows, block):
    near_c, near_s = near_ref[0, rows, :], near_ref[1, rows, :]
    base_c, base_s = base_ref[0, pl.ds(block, 1), :], base_ref[1, pl.ds(block, 1), :]
    return near_c * base_c - near_s * base_s, near_s * base_c + near_c * base_s


def turn(value, cosine, sine):
    return value * cosine + pltpu.roll(value, HEAD_DIM // 2, 1) * sine


def turn_back(value, cosine, sine):
    return value * cosine - pltpu.roll(value, HEAD_DIM // 2, 1) * sine


def head(index):
    return slice(index * HEAD_DIM, (index + 1) * HEAD_DIM)


def split(value):
    high = value.astype(BF).astype(F32)
    return high, value - high


def tiles(value, scratch):
    for k in range(8):
        scratch[k : k + 1, :] = value[:, k * 128 : (k + 1) * 128]
    return scratch[...]


def halve(value, step, count, keep_ref, send_ref):
    bit = (lax.axis_index("seq") // step) % 2
    keep_ref[...] = value[pl.ds(pl.multiple_of(bit * count, count), count), :]
    send_ref[...] = value[pl.ds(pl.multiple_of((1 - bit) * count, count), count), :].astype(BF)


def tables_kernel(*refs):
    prev_ref, sources, (out_ref,) = refs[0], refs[1:11], refs[11:12]
    near_ref, base_ref, ids_ref, gain_ref, emb, wk, wv, wq, do, wo = refs[12:22]
    tab, q_ref, k_ref, v_ref, ga_ref, kprev, vprev, vtab, gq, kg, vg, sems = refs[22:]
    kept = (emb, near_ref, base_ref, ids_ref, gain_ref, wk, wv, wq, do, wo)
    copies = [pltpu.make_async_copy(s, d, sems.at[i]) for i, (s, d) in enumerate(zip(sources, kept))]
    for copy in copies:
        copy.start()
    block = lax.axis_index("seq")
    place = lax.broadcasted_iota(jnp.int32, (VOCAB, VOCAB), 0)
    value = lax.broadcasted_iota(jnp.int32, (VOCAB, VOCAB), 1)
    order = (table_row(value) == place).astype(F32).astype(BF)
    for copy in copies[:5]:
        copy.wait()
    hot_own, hot_prev = hot_columns(ids_ref[...]), hot_columns(prev_ref[...])
    cos_p, sin_p = turn_tables(near_ref, base_ref, slice(0, TOK), block)
    cos_o, sin_o = turn_tables(near_ref, base_ref, slice(TOK, 2 * TOK), block)
    inputs = mm(order, emb[...])
    recip = lax.rsqrt(jnp.mean(inputs * inputs, axis=-1, keepdims=True) + EPSILON)
    normed = (inputs * recip * gain_ref[...]).astype(BF)

    def fill(weight):
        full = mm(normed, weight[...])
        high = full.astype(BF)
        tab[:VOCAB, :] = high
        tab[VOCAB:, :] = (full - high.astype(F32)).astype(BF)

    def gather(hot, cosine, sine, out_ref):
        full = mm_tn(jnp.concatenate([hot, hot], axis=0), tab[...])
        for h in range(HEADS):
            out_ref[:, head(h)] = turn(full[:, head(h)], cosine, sine).astype(BF)

    copies[5].wait()
    fill(wk)
    gather(hot_own, cos_o, sin_o, k_ref)
    gather(hot_prev, cos_p, sin_p, kprev)
    copies[6].wait()
    vtab[...] = mm(normed, wv[...]).astype(BF)
    v_ref[...] = mm_tn(hot_own, vtab[...]).astype(BF)
    vprev[...] = mm_tn(hot_prev, vtab[...]).astype(BF)
    copies[7].wait()
    fill(wq)
    gather(hot_own, cos_o, sin_o, q_ref)
    copies[8].wait()
    copies[9].wait()
    ga_ref[...] = mm(do[...], wo[...]).astype(BF)
    lead = jnp.where(block == 0, NEGATIVE, 0.0).astype(F32)
    scale = HEAD_DIM ** (-0.5)
    own = lax.broadcasted_iota(jnp.int32, (TOK, TOK), 0) <= lax.broadcasted_iota(
        jnp.int32, (TOK, TOK), 1
    )
    for h in range(HEADS):
        query, grad = q_ref[:, head(h)], ga_ref[:, head(h)]
        key_o, key_p = k_ref[:, head(h)], kprev[:, head(h)]
        value_o, value_p = v_ref[:, head(h)], vprev[:, head(h)]
        scores = jnp.where(own, mm_nt(key_o, query), mm_nt(key_p, query) + lead)
        highest = jnp.max(scores, axis=0, keepdims=True)
        weights = jnp.exp((scores - highest) * scale)
        probs = weights * (1.0 / jnp.sum(weights, axis=0, keepdims=True))
        grad_probs = jnp.where(own, mm_nt(value_o, grad), mm_nt(value_p, grad))
        delta = jnp.sum(probs * grad_probs, axis=0, keepdims=True)
        grad_scores = probs * (grad_probs - delta) * scale
        probs_o = jnp.where(own, probs, 0.0).astype(BF)
        probs_p = jnp.where(own, 0.0, probs).astype(BF)
        gs_o = jnp.where(own, grad_scores, 0.0).astype(BF)
        gs_p = jnp.where(own, 0.0, grad_scores).astype(BF)
        vg[:TOK, head(h)] = mm(probs_p, grad).astype(BF)
        vg[TOK:, head(h)] = mm(probs_o, grad).astype(BF)
        kg[:TOK, head(h)] = turn_back(mm(gs_p, query), cos_p, sin_p).astype(BF)
        kg[TOK:, head(h)] = turn_back(mm(gs_o, query), cos_o, sin_o).astype(BF)
        grad_q = mm_tn(gs_o, key_o) + mm_tn(gs_p, key_p)
        gq[:, head(h)] = turn_back(grad_q, cos_o, sin_o).astype(BF)
    hot2 = jnp.concatenate([hot_prev, hot_own], axis=1)
    key_table = mm(hot2, kg[...]).astype(BF)
    out_ref[:, :, :D] = key_table.reshape(PLANE, RING, D)
    value_table = mm(hot2, vg[...]).astype(BF)
    query_table = mm(hot_own, gq[...]).astype(BF)
    grad_normed = mm_nt(key_table, wk[...]) + mm_nt(value_table, wv[...]) + mm_nt(query_table, wq[...])
    out_ref[:, :, D : 2 * D] = grad_normed.astype(BF).reshape(PLANE, RING, D)


def rows_kernel(emb_ref, gain_ref, pick_ref, row_ref, scaled_ref, rows):
    block, lane = lax.axis_index("seq"), lax.axis_index("dp")
    ring = lax.rem(block, RING)
    index = lax.broadcasted_iota(jnp.int32, (RING, VOCAB), 0)
    value = lax.broadcasted_iota(jnp.int32, (RING, VOCAB), 1)
    mine = value == (block - ring + index) * N + lane
    rows[...] = mm(mine.astype(F32).astype(BF), emb_ref[...])
    inputs = rows[...]
    recip = lax.rsqrt(jnp.mean(inputs * inputs, axis=-1, keepdims=True) + EPSILON)
    scaled_ref[...] = inputs * recip
    normed = (scaled_ref[...] * gain_ref[...]).astype(BF)
    place = lax.broadcasted_iota(jnp.int32, (D, 256), 1)
    member = place >> 3
    column = ((member >> 4) << 9) + ring * 64 + ((member & 15) << 2) + (place & 3)
    choose = (lax.broadcasted_iota(jnp.int32, (D, 256), 0) == column).astype(F32).astype(BF)
    picked = mm(normed, choose)
    pick_ref[...] = jnp.concatenate([picked, picked], axis=0).astype(BF)
    row_ref[...] = rows[pl.ds(ring, 1), :]


def share(keep_ref, send_ref):
    high, low = split(keep_ref[:, 2 * D : 2 * D + 128] + keep_ref[:, 2 * D + 128 :])
    keep_ref[:, 2 * D : 2 * D + 128] = high
    keep_ref[:, 2 * D + 128 :] = low
    send_ref[...] = keep_ref[...].astype(BF)


def first_kernel(got_ref, scaled_ref, keep_ref, send_ref, terms):
    total = jnp.sum(got_ref[...].astype(F32), axis=0)
    keep_ref[:, : 2 * D] = total
    product = jnp.sum(total[:, D:] * scaled_ref[...], axis=0, keepdims=True)
    keep_ref[:, 2 * D : 2 * D + 128] = tiles(product, terms)
    keep_ref[:, 2 * D + 128 :] = jnp.zeros((RING, 128), F32)
    share(keep_ref, send_ref)


def total_of(kept_ref, got, columns):
    total = kept_ref[:, columns]
    for ref in got:
        total = total + ref[:, columns].astype(F32)
    return total


def round_kernel(kept_ref, *refs):
    got, (keep_ref, send_ref) = refs[:-2], refs[-2:]
    keep_ref[...] = total_of(kept_ref, got, slice(None))
    share(keep_ref, send_ref)


def weight_kernel(kept_ref, *refs):
    got, (pick_ref, out_ref) = refs[:-2], refs[-2:]
    both = jnp.concatenate(split(total_of(kept_ref, got, slice(0, D))), axis=0).astype(BF)
    part = mm_tn(pick_ref[...], both)
    first = (lax.broadcasted_iota(jnp.int32, (256, 512), 0) & 4) == 0
    part = jnp.where(first, part[:, :512], part[:, 512:])
    out_ref[:, :, :512] = part.reshape(PLANE, 8, 512).astype(BF)
    terms = total_of(kept_ref, got, slice(2 * D, WIDE))
    terms = terms[:, :128] + terms[:, 128:]
    out_ref[:, :, 512:] = jnp.broadcast_to(terms.astype(BF)[None], (PLANE, 8, 128))


def row_kernel(kept_ref, *refs):
    got, (row_ref, gain_ref, ge_ref, rows) = refs[:-4], refs[-4:]
    rows[...] = total_of(kept_ref, got, slice(D, 2 * D))
    grad_normed = rows[pl.ds(lax.rem(lax.axis_index("seq"), RING), 1), :]
    inputs = row_ref[...]
    recip = lax.rsqrt(jnp.mean(inputs * inputs, axis=-1, keepdims=True) + EPSILON)
    grad_scaled = grad_normed * gain_ref[...]
    inner = jnp.mean(grad_scaled * inputs, axis=-1, keepdims=True)
    ge_ref[...] = recip * grad_scaled - inputs * (recip * recip * recip) * inner


def finish_kernel(got_ref, gk_ref, gg_ref):
    total = jnp.sum(got_ref[...].astype(F32), axis=0)
    gk_ref[:, :512] = total[:4, :512]
    gk_ref[:, 512:] = total[4:, :512]
    start = (lax.axis_index("seq") * N + lax.axis_index("dp")) * 4
    mine = lax.broadcasted_iota(jnp.int32, (8, 128), 0) == start // 128
    row = jnp.sum(jnp.where(mine, total[:, 512:], 0.0), axis=0, keepdims=True)
    gg_ref[...] = pltpu.roll(jnp.broadcast_to(row, (8, 128)), 128 - lax.rem(start, 128), 1)


def call(kernel, outs, ins, scratch=(), flops=0, moved=0, limit=16):
    far_space = pl.BlockSpec(memory_space=pltpu.HBM)
    vmem = pl.BlockSpec(memory_space=pltpu.VMEM)
    return pl.pallas_call(
        kernel,
        out_shape=[jax.ShapeDtypeStruct(shape, kind) for shape, kind in outs],
        in_specs=[far_space if far else vmem for _, far in ins],
        out_specs=[vmem] * len(outs),
        scratch_shapes=list(scratch),
        compiler_params=pltpu.CompilerParams(vmem_limit_bytes=limit * MIB),
        cost_estimate=pl.CostEstimate(flops=flops, bytes_accessed=moved, transcendentals=0),
    )(*[value for value, _ in ins])


def local(byte_ids, embedding, gain, w_query, w_key, w_value, w_out, d_output):
    near_table, base_table = (jnp.asarray(table) for table in angle_tables())
    prev_ids = lax.ppermute(byte_ids, "seq", [(i, i + 1) for i in range(N - 1)])
    gain_row = gain.reshape(1, D)
    mat = pltpu.VMEM((D, D), BF)
    tall = pltpu.VMEM((2 * TOK, D), BF)
    flat = pltpu.VMEM((TOK, D), BF)
    near = lambda *values: [(value, False) for value in values]
    far = lambda *values: [(value, True) for value in values]
    (tables,) = call(
        tables_kernel,
        [((PLANE, RING, 2 * D), BF)],
        near(prev_ids)
        + far(embedding, near_table, base_table, byte_ids, gain_row)
        + far(w_key, w_value, w_query, d_output[0], w_out),
        [
            pltpu.VMEM((2, 2 * TOK, 128), F32),
            pltpu.VMEM((2, N, 128), F32),
            pltpu.VMEM((1, TOK), jnp.int32),
            pltpu.VMEM((1, D), F32),
            *[flat, mat, mat, mat, flat, mat, tall],
            *[flat] * 8,
            *[tall, tall],
            pltpu.SemaphoreType.DMA((10,)),
        ],
        flops=8_000_000_000,
        moved=14_000_000,
        limit=56,
    )
    parts = exchange(tables)
    embedding_later, _ = lax.optimization_barrier((embedding, tables))
    pick, row, scaled = call(
        rows_kernel,
        [((16, 256), BF), ((1, D), F32), ((RING, D), F32)],
        near(embedding_later, gain_row),
        [pltpu.VMEM((RING, D), F32)],
        flops=10_000_000,
        moved=600_000,
    )
    both = [((RING, WIDE), F32), ((RING, WIDE), BF)]
    kept, sent = call(
        first_kernel,
        both,
        near(parts, scaled),
        [pltpu.VMEM((8, 128), F32)],
        flops=1_000_000,
        moved=1_300_000,
    )
    for steps in ROUNDS[:-1]:
        got = [swap(sent, step) for step in steps]
        kept, sent = call(round_kernel, both, near(kept, *got), flops=1_000_000, moved=600_000)
    got = [swap(sent, step) for step in ROUNDS[-1]]
    (part,) = call(
        weight_kernel, [((PLANE, 8, 640), BF)], near(kept, *got, pick), flops=10_000_000, moved=400_000
    )
    parts = exchange(part)
    (grad_row,) = call(
        row_kernel,
        [((1, D), F32)],
        near(kept, *got, row, gain_row),
        [pltpu.VMEM((RING, D), F32)],
        flops=1_000_000,
        moved=300_000,
    )
    grad_weight, gain_own = call(
        finish_kernel,
        [((4, D), F32), ((8, 128), F32)],
        near(parts),
        flops=1_000_000,
        moved=200_000,
    )
    return grad_weight, gain_own[0, :4], grad_row


def solution(mesh):
    in_specs = (P("dp", "seq"), P(), P(), P(), P(), P(), P(), P("dp", "seq", None))
    out_specs = (P(("seq", "dp"), None), P(("seq", "dp")), P(("seq", "dp"), None))
    return jax.shard_map(local, mesh=mesh, in_specs=in_specs, out_specs=out_specs, check_vma=False)
```

time: 89.9 us -> 85.1 us (0.947)
  blocking collectives: 16 us -> 0 us
  waiting for transfers between devices: 24.5 us -> 36 us
  starting transfers between devices: 18.2 us -> 29.1 us
  Pallas kernels: 26.4 us -> 17.8 us
  local copies, waits for them, and re-layouts: 3.52 us -> 1.08 us
    all_to_all x1 -> x0, blocking collectives: 16 us -> none  [exchange(): lax.all_to_all(value, AXES, 0, 0, axis_index_groups=groups, tiled=False)]
    ppermute x1 -> x4, waiting for transfers between devices: 0.01 us -> 10.4 us  [the longest x3 9.53 us: swap(): return lax.ppermute(value, 'seq', [(i, i ^ step) for i in range(N)])]
    pallas_call x6 -> x8, Pallas kernels: 26.4 us -> 17.8 us  [call(): pl.pallas_call(kernel, out_shape=[jax.ShapeDtypeStruct(shape, kind) for s...]
    all_to_all x2, starting transfers between devices: 13.8 us -> 20.7 us  [exchange(): lax.all_to_all(value, ('seq', 'dp'), 0, 0, axis_index_groups=groups, tile...]
    ppermute x1 -> x4, starting transfers between devices: 4.37 us -> 8.44 us  [the longest x1 4.37 us: local(): prev_ids = lax.ppermute(byte_ids, 'seq', [(i, i + 1) for i in range(N - 1)])]
    unnamed x6, local copies, waits for them, and re-layouts: 2.25 us -> 0.57 us
    dynamic_slice x1 -> x0, local copies, waits for them, and re-layouts: 1.26 us -> none  [local(): lax.dynamic_slice(gg.reshape(D), ((block * N_DP + lane) * 4,), (4,))]
    all_to_all x2, waiting for transfers between devices: 24.5 us -> 25.5 us  [exchange(): lax.all_to_all(value, ('seq', 'dp'), 0, 0, axis_index_groups=groups, tile...]
  transfers between devices with their start and end apart: 3 -> 6, of which waited for: 2 -> 6; matrix products, arithmetic and copies ran while one was open for 0% -> 0% of each run, Pallas kernels for 11% -> 1%
where the time goes in v2:
time: 85.1 us; the launch traced here: 84.8 us
  waiting for transfers between devices  36 us (42%)
  starting transfers between devices  29.1 us (34%)
  Pallas kernels  17.8 us (21%)
  local copies, waits for them, and re-layouts  1.08 us (1%)
    all_to_all x2, waiting for transfers between devices, exchange(): lax.all_to_all(value, ('seq', 'dp'), 0, 0, axis_index_groups=groups, tile...  25.5 us
    all_to_all x2, starting transfers between devices, exchange(): lax.all_to_all(value, ('seq', 'dp'), 0, 0, axis_index_groups=groups, tile...  20.7 us
    pallas_call x8, Pallas kernels, call(): pl.pallas_call(kernel, out_shape=[jax.ShapeDtypeStruct(shape, kind) for s...  17.8 us
    ppermute x3, waiting for transfers between devices, swap(): return lax.ppermute(value, 'seq', [(i, i ^ step) for i in range(N)])  9.53 us
    ppermute x1, starting transfers between devices, local(): prev_ids = lax.ppermute(byte_ids, 'seq', [(i, i + 1) for i in range(N - 1)])  4.37 us
    ppermute x3, starting transfers between devices, swap(): return lax.ppermute(value, 'seq', [(i, i ^ step) for i in range(N)])  4.06 us
  transfers between devices with their start and end apart: 6, of which 6 were waited for; matrix products, arithmetic and copies ran while one was open for 0% of the time, Pallas kernels for 1%

profile of v2, /device:TPU:1, one launch (start us, length us, event | category | flops | bytes accessed | tf_op | source)
XLA Modules:
  0.0 84.8 jit_solution(1594445420693367692)
XLA Ops:
  0.6 4.4 %collective-permute-start = (s32[1,256]{1,0:T(1,128)}, s32[1,256]{1,0:T(1,128)S(1)}, u32[]{:S(2)}, u32[]{:S(2)}) collective-permute-start(s32[1,256]{1,0:T(1,128)} %refs_4_.1), channel_id=1, source_target_pairs={{0,16},{16,32},{32,48},{48,64},{64,80},{80,96},{96,112},{112,128},... | collective-permute-start | bytes 3080 | tf_op jit(solution)/shard_map/ppermute | solution.py:286
  5.0 0.9 %collective-permute-done.refs_0_ = s32[1,256]{1,0:T(1,128)S(1)} collective-permute-done((s32[1,256]{1,0:T(1,128)}, s32[1,256]{1,0:T(1,128)S(1)}, u32[]{:S(2)}, u32[]{:S(2)}) %collective-permute-start) | collective-permute-done | bytes 1056 | tf_op jit(solution)/shard_map/ppermute | solution.py:286
  5.9 0.0 copy-start.2
  5.9 0.6 copy-done.2
  6.5 14.6 %shard_map.121 = bf16[32,8,2048]{2,1,0:T(8,128)(2,1)} custom-call(s32[1,256]{1,0:T(1,128)} %copy-done.2, bf16[256,1024]{1,0:T(8,128)(2,1)} %emb_ref, f32[2,512,128]{2,1,0:T(8,128)} %constant.4.clone.refs_2_, f32[2,16,128]{2,1,0:T(8,128)} %constant.5.clone.refs_3_, s32[1,256]{1,0:T(1,128)} %refs_4_.1, f32[1,1024]{1,0:T(1,128)} %bitcast.4, ...), custom_call_target="tpu_custom_call" | custom-call | flops 8000000000 | bytes 14000000 | tf_op jit(solution)/shard_map/pallas_call | solution.py:273
  21.1 0.0 copy-start
  21.1 0.0 copy-start.1
  21.2 13.4 %all-to-all-start = ((bf16[32,8,2048]{2,1,0:T(8,128)(2,1)}), bf16[32,8,2048]{2,1,0:T(8,128)(2,1)S(1)}, u32[]{:S(2)}, u32[]{:S(2)}) async-start(bf16[32,8,2048]{2,1,0:T(8,128)(2,1)} %shard_map.121), calls=%async_computation | async-start | bytes 2097152 | tf_op jit(solution)/shard_map/all_to_all | solution.py:30
  34.6 0.0 copy-done
  34.6 0.0 copy-done.1
  34.6 0.5 shard_map.122
  35.2 16.6 %all-to-all-done.got_ref = bf16[32,8,2048]{2,1,0:T(8,128)(2,1)S(1)} async-done(((bf16[32,8,2048]{2,1,0:T(8,128)(2,1)}), bf16[32,8,2048]{2,1,0:T(8,128)(2,1)S(1)}, u32[]{:S(2)}, u32[]{:S(2)}) %all-to-all-start) | async-done | bytes 1048608 | tf_op jit(solution)/shard_map/all_to_all | solution.py:30
  51.8 0.2 shard_map.123
  52.0 0.1 collective-permute-start.1
  52.1 2.8 %collective-permute-done.1.refs_0_ = bf16[8,2304]{1,0:T(8,128)(2,1)S(1)} collective-permute-done((bf16[8,2304]{1,0:T(8,128)(2,1)S(1)}, bf16[8,2304]{1,0:T(8,128)(2,1)S(1)}, u32[]{:S(2)}, u32[]{:S(2)}) %collective-permute-start.1) | collective-permute-done | bytes 36896 | tf_op jit(solution)/shard_map/ppermute | solution.py:34
  54.9 0.1 collective-permute-start.2
  55.0 3.8 %collective-permute-done.2.refs_0_ = bf16[8,2304]{1,0:T(8,128)(2,1)S(1)} collective-permute-done((bf16[8,2304]{1,0:T(8,128)(2,1)S(1)}, bf16[8,2304]{1,0:T(8,128)(2,1)S(1)}, u32[]{:S(2)}, u32[]{:S(2)}) %collective-permute-start.2) | collective-permute-done | bytes 36896 | tf_op jit(solution)/shard_map/ppermute | solution.py:34
  58.8 3.9 %collective-permute-start.3 = (bf16[8,2304]{1,0:T(8,128)(2,1)S(1)}, bf16[8,2304]{1,0:T(8,128)(2,1)S(1)}, u32[]{:S(2)}, u32[]{:S(2)}) collective-permute-start(bf16[8,2304]{1,0:T(8,128)(2,1)S(1)} %get-tuple-element.22), channel_id=1, source_target_pairs={{0,64},{16,80},{32,96},{48,112},{64,0},{80,16},{96,32},{112,48},{1... | collective-permute-start | bytes 110600 | tf_op jit(solution)/shard_map/ppermute | solution.py:34
  62.7 2.9 %collective-permute-done.3.refs_0_ = bf16[8,2304]{1,0:T(8,128)(2,1)S(1)} collective-permute-done((bf16[8,2304]{1,0:T(8,128)(2,1)S(1)}, bf16[8,2304]{1,0:T(8,128)(2,1)S(1)}, u32[]{:S(2)}, u32[]{:S(2)}) %collective-permute-start.3) | collective-permute-done | bytes 36896 | tf_op jit(solution)/shard_map/ppermute | solution.py:34
  65.6 1.0 %shard_map.126 = bf16[32,8,640]{2,1,0:T(8,128)(2,1)} custom-call(f32[8,2304]{1,0:T(8,128)S(1)} %get-tuple-element.21.kept_ref, bf16[8,2304]{1,0:T(8,128)(2,1)S(1)} %collective-permute-done.3.refs_0_, bf16[16,256]{1,0:T(8,128)(2,1)S(1)} %get-tuple-element.23.refs_1_), custom_call_target="tpu_custom_call" | custom-call | flops 10000000 | bytes 400000 | tf_op jit(solution)/shard_map/pallas_call | solution.py:273
  66.7 7.2 %all-to-all-start.1 = ((bf16[32,8,640]{2,1,0:T(8,128)(2,1)}), bf16[32,8,640]{2,1,0:T(8,128)(2,1)S(1)}, u32[]{:S(2)}, u32[]{:S(2)}) async-start(bf16[32,8,640]{2,1,0:T(8,128)(2,1)} %shard_map.126), calls=%async_computation.1 | async-start | bytes 655360 | tf_op jit(solution)/shard_map/all_to_all | solution.py:30
  73.9 0.7 shard_map.128
  74.6 8.9 %all-to-all-done.1.got_ref = bf16[32,8,640]{2,1,0:T(8,128)(2,1)S(1)} async-done(((bf16[32,8,640]{2,1,0:T(8,128)(2,1)}), bf16[32,8,640]{2,1,0:T(8,128)(2,1)S(1)}, u32[]{:S(2)}, u32[]{:S(2)}) %all-to-all-start.1) | async-done | bytes 327712 | tf_op jit(solution)/shard_map/all_to_all | solution.py:30
  83.6 0.7 shard_map.127
  84.2 0.5 slice_bitcast_fusion
  (2 shorter events, 0.0 us)
Async XLA Ops:
  0.6 5.3 %collective-permute-start = (s32[1,256]{1,0:T(1,128)}, s32[1,256]{1,0:T(1,128)S(1)}, u32[]{:S(2)}, u32[]{:S(2)}) collective-permute-start(s32[1,256]{1,0:T(1,128)} %refs_4_.1), channel_id=1, source_target_pairs={{0,16},{16,32},{32,48},{48,64},{64,80},{80,96},{96,112},{112,128},... | collective-permute-start | bytes 3080 | tf_op jit(solution)/shard_map/ppermute | solution.py:286
  5.9 0.6 copy-start.2
  21.1 13.5 %copy-start = (bf16[256,1024]{1,0:T(8,128)(2,1)S(1)}, bf16[256,1024]{1,0:T(8,128)(2,1)}, u32[]{:S(2)}) copy-start(bf16[256,1024]{1,0:T(8,128)(2,1)} %emb_ref) | copy-start | bytes 1572868
  21.1 13.5 %copy-start.1 = (f32[1024]{0:T(1024)S(1)}, f32[1024]{0:T(1024)}, u32[]{:S(2)}) copy-start(f32[1024]{0:T(1024)} %param.12) | copy-start | bytes 12292
  21.2 30.6 %all-to-all-start = ((bf16[32,8,2048]{2,1,0:T(8,128)(2,1)}), bf16[32,8,2048]{2,1,0:T(8,128)(2,1)S(1)}, u32[]{:S(2)}, u32[]{:S(2)}) async-start(bf16[32,8,2048]{2,1,0:T(8,128)(2,1)} %shard_map.121), calls=%async_computation | async-start | bytes 2097152 | tf_op jit(solution)/shard_map/all_to_all | solution.py:30
  52.0 2.9 %collective-permute-start.1 = (bf16[8,2304]{1,0:T(8,128)(2,1)S(1)}, bf16[8,2304]{1,0:T(8,128)(2,1)S(1)}, u32[]{:S(2)}, u32[]{:S(2)}) collective-permute-start(bf16[8,2304]{1,0:T(8,128)(2,1)S(1)} %get-tuple-element.18), channel_id=1, source_target_pairs={{0,16},{16,0},{32,48},{48,32},{64,80},{80,64},{96,112},{112,96},{1... | collective-permute-start | bytes 110600 | tf_op jit(solution)/shard_map/ppermute | solution.py:34
  54.9 3.9 %collective-permute-start.2 = (bf16[8,2304]{1,0:T(8,128)(2,1)S(1)}, bf16[8,2304]{1,0:T(8,128)(2,1)S(1)}, u32[]{:S(2)}, u32[]{:S(2)}) collective-permute-start(bf16[8,2304]{1,0:T(8,128)(2,1)S(1)} %get-tuple-element.20), channel_id=1, source_target_pairs={{0,32},{16,48},{32,0},{48,16},{64,96},{80,112},{96,64},{112,80},{1... | collective-permute-start | bytes 110600 | tf_op jit(solution)/shard_map/ppermute | solution.py:34
  58.8 6.8 %collective-permute-start.3 = (bf16[8,2304]{1,0:T(8,128)(2,1)S(1)}, bf16[8,2304]{1,0:T(8,128)(2,1)S(1)}, u32[]{:S(2)}, u32[]{:S(2)}) collective-permute-start(bf16[8,2304]{1,0:T(8,128)(2,1)S(1)} %get-tuple-element.22), channel_id=1, source_target_pairs={{0,64},{16,80},{32,96},{48,112},{64,0},{80,16},{96,32},{112,48},{1... | collective-permute-start | bytes 110600 | tf_op jit(solution)/shard_map/ppermute | solution.py:34
  66.7 16.9 %all-to-all-start.1 = ((bf16[32,8,640]{2,1,0:T(8,128)(2,1)}), bf16[32,8,640]{2,1,0:T(8,128)(2,1)S(1)}, u32[]{:S(2)}, u32[]{:S(2)}) async-start(bf16[32,8,640]{2,1,0:T(8,128)(2,1)} %shard_map.126), calls=%async_computation.1 | async-start | bytes 655360 | tf_op jit(solution)/shard_map/all_to_all | solution.py:30

commit v3 on v2

v3 whole, which is shorter than its diff:
```python
import functools

import jax
import jax.numpy as jnp
import numpy as np
from jax import lax
from jax.experimental import pallas as pl
from jax.experimental.pallas import tpu as pltpu
from jax.sharding import PartitionSpec as P

HEADS = 8
HEAD_DIM = 128
D = 1024
VOCAB = 256
TOK = 256
N = 16
NEGATIVE = -1e30
EPSILON = 1e-05
THETA = 10000.0
BF = jnp.bfloat16
F32 = jnp.float32
MIB = 1024 * 1024

WIDE = 2 * D + 128
KEYS = D + 128
ROUNDS = ((1, 4, 4, 256), (8, 2, 2, 128), (4, 2, 1, 128))


def exchange(value, axis):
    return lax.all_to_all(value, axis, 0, 0, tiled=False)


def swap(value, step):
    return lax.ppermute(value, "seq", [(i, i ^ step) for i in range(N)])


def angle_tables():
    inverse = THETA ** (-np.arange(HEAD_DIM // 2, dtype=np.float64) / (HEAD_DIM // 2))
    near = np.arange(-TOK, TOK, dtype=np.float64)[:, None] * inverse[None, :]
    base = (TOK * np.arange(16, dtype=np.float64))[:, None] * inverse[None, :]

    def wide(angle):
        cosine, sine = np.cos(angle), np.sin(angle)
        return np.stack(
            [np.concatenate([cosine, cosine], -1), np.concatenate([-sine, sine], -1)]
        ).astype(np.float32)

    return wide(near), wide(base)


def mm(left, right):
    return lax.dot_general(left, right, (((1,), (0,)), ((), ())), preferred_element_type=F32)


def mm_nt(left, right):
    return lax.dot_general(left, right, (((1,), (1,)), ((), ())), preferred_element_type=F32)


def mm_tn(left, right):
    return lax.dot_general(left, right, (((0,), (0,)), ((), ())), preferred_element_type=F32)


def table_row(ids):
    return ((ids & 15) << 4) | (((ids >> 4) & 3) << 2) | (ids >> 6)


def hot_columns(ids_row):
    place = lax.broadcasted_iota(jnp.int32, (VOCAB, TOK), 0)
    return (place == table_row(ids_row)).astype(F32).astype(BF)


def turn_tables(near_ref, base_ref, rows, block):
    near_c, near_s = near_ref[0, rows, :], near_ref[1, rows, :]
    base_c, base_s = base_ref[0, pl.ds(block, 1), :], base_ref[1, pl.ds(block, 1), :]
    return near_c * base_c - near_s * base_s, near_s * base_c + near_c * base_s


def turn(value, cosine, sine):
    return value * cosine + pltpu.roll(value, HEAD_DIM // 2, 1) * sine


def turn_back(value, cosine, sine):
    return value * cosine - pltpu.roll(value, HEAD_DIM // 2, 1) * sine


def head(index):
    return slice(index * HEAD_DIM, (index + 1) * HEAD_DIM)


def split(value):
    high = value.astype(BF).astype(F32)
    return high, value - high


def tiles(value, scratch):
    for k in range(8):
        scratch[k : k + 1, :] = value[:, k * 128 : (k + 1) * 128]
    return scratch[...]


def halve(value, step, count, keep_ref, send_ref):
    bit = (lax.axis_index("seq") // step) % 2
    keep_ref[...] = value[pl.ds(pl.multiple_of(bit * count, count), count), :]
    send_ref[...] = value[pl.ds(pl.multiple_of((1 - bit) * count, count), count), :].astype(BF)


def tables_kernel(*refs):
    prev_ref, sources, (out_ref,) = refs[0], refs[1:11], refs[11:12]
    near_ref, base_ref, ids_ref, gain_ref, emb, wk, wv, wq, do, wo = refs[12:22]
    tab, q_ref, k_ref, v_ref, ga_ref, kprev, vprev, vtab, gq, kg, vg, scaled, terms, sems = refs[22:]
    kept = (emb, near_ref, base_ref, ids_ref, gain_ref, wk, wv, wq, do, wo)
    copies = [pltpu.make_async_copy(s, d, sems.at[i]) for i, (s, d) in enumerate(zip(sources, kept))]
    for copy in copies:
        copy.start()
    block = lax.axis_index("seq")
    place = lax.broadcasted_iota(jnp.int32, (VOCAB, VOCAB), 0)
    value = lax.broadcasted_iota(jnp.int32, (VOCAB, VOCAB), 1)
    order = (table_row(value) == place).astype(F32).astype(BF)
    for copy in copies[:5]:
        copy.wait()
    hot_own, hot_prev = hot_columns(ids_ref[...]), hot_columns(prev_ref[...])
    rows_own, rows_prev = hot_own.T, hot_prev.T
    cos_p, sin_p = turn_tables(near_ref, base_ref, slice(0, TOK), block)
    cos_o, sin_o = turn_tables(near_ref, base_ref, slice(TOK, 2 * TOK), block)
    inputs = mm(order, emb[...])
    recip = lax.rsqrt(jnp.mean(inputs * inputs, axis=-1, keepdims=True) + EPSILON)
    scaled[...] = inputs * recip
    normed = (scaled[...] * gain_ref[...]).astype(BF)

    def fill(weight):
        full = mm(normed, weight[...])
        high = full.astype(BF)
        tab[:VOCAB, :] = high
        tab[VOCAB:, :] = (full - high.astype(F32)).astype(BF)

    def gather(hot, cosine, sine, out_ref):
        full = mm(jnp.concatenate([hot, hot], axis=1), tab[...])
        for h in range(HEADS):
            out_ref[:, head(h)] = turn(full[:, head(h)], cosine, sine).astype(BF)

    copies[5].wait()
    fill(wk)
    gather(rows_own, cos_o, sin_o, k_ref)
    gather(rows_prev, cos_p, sin_p, kprev)
    copies[6].wait()
    vtab[...] = mm(normed, wv[...]).astype(BF)
    v_ref[...] = mm(rows_own, vtab[...]).astype(BF)
    vprev[...] = mm(rows_prev, vtab[...]).astype(BF)
    copies[7].wait()
    fill(wq)
    gather(rows_own, cos_o, sin_o, q_ref)
    copies[8].wait()
    copies[9].wait()
    ga_ref[...] = mm(do[...], wo[...]).astype(BF)
    lead = jnp.where(block == 0, NEGATIVE, 0.0).astype(F32)
    scale = HEAD_DIM ** (-0.5)
    own = lax.broadcasted_iota(jnp.int32, (TOK, TOK), 0) <= lax.broadcasted_iota(
        jnp.int32, (TOK, TOK), 1
    )
    behind_o = own.astype(F32).T.astype(BF)
    behind_p = 1 - behind_o
    for h in range(HEADS):
        query, grad = q_ref[:, head(h)], ga_ref[:, head(h)]
        key_o, key_p = k_ref[:, head(h)], kprev[:, head(h)]
        value_o, value_p = v_ref[:, head(h)], vprev[:, head(h)]
        scores = jnp.where(own, mm_nt(key_o, query), mm_nt(key_p, query) + lead)
        highest = jnp.max(scores, axis=0, keepdims=True)
        weights = jnp.exp((scores - highest) * scale)
        probs = weights * (1.0 / jnp.sum(weights, axis=0, keepdims=True))
        grad_probs = jnp.where(own, mm_nt(value_o, grad), mm_nt(value_p, grad))
        delta = jnp.sum(probs * grad_probs, axis=0, keepdims=True)
        grad_scores = probs * (grad_probs - delta) * scale
        probs_o = jnp.where(own, probs, 0.0).astype(BF)
        probs_p = jnp.where(own, 0.0, probs).astype(BF)
        gs_o = jnp.where(own, grad_scores, 0.0).astype(BF)
        gs_p = jnp.where(own, 0.0, grad_scores).astype(BF)
        turned = grad_scores.astype(BF).T
        vg[:TOK, head(h)] = mm(probs_p, grad).astype(BF)
        vg[TOK:, head(h)] = mm(probs_o, grad).astype(BF)
        kg[:TOK, head(h)] = turn_back(mm(gs_p, query), cos_p, sin_p).astype(BF)
        kg[TOK:, head(h)] = turn_back(mm(gs_o, query), cos_o, sin_o).astype(BF)
        grad_q = mm(turned * behind_o, key_o) + mm(turned * behind_p, key_p)
        gq[:, head(h)] = turn_back(grad_q, cos_o, sin_o).astype(BF)
    hot2 = jnp.concatenate([hot_prev, hot_own], axis=1)
    key_table = mm(hot2, kg[...]).astype(BF)
    out_ref[:, :, :D] = key_table.reshape(N, N, D)
    value_table = mm(hot2, vg[...]).astype(BF)
    query_table = mm(hot_own, gq[...]).astype(BF)
    grad_normed = mm_nt(key_table, wk[...]) + mm_nt(value_table, wv[...]) + mm_nt(query_table, wq[...])
    out_ref[:, :, D : 2 * D] = grad_normed.astype(BF).reshape(N, N, D)
    product = jnp.sum(grad_normed * scaled[...], axis=0, keepdims=True)
    gain_terms = jnp.concatenate(split(tiles(product, terms)), axis=0).astype(BF)
    out_ref[:, :, 2 * D :] = jnp.broadcast_to(gain_terms[None], (N, N, 128))


def rows_kernel(emb_ref, gain_ref, pick_ref, row_ref):
    block, lane = lax.axis_index("seq"), lax.axis_index("dp")
    index = lax.broadcasted_iota(jnp.int32, (2 * N, VOCAB), 0)
    value = lax.broadcasted_iota(jnp.int32, (2 * N, VOCAB), 1)
    wanted = jnp.where(index < N, N * lane + index, table_row(N * block + lane))
    inputs = mm((table_row(value) == wanted).astype(F32).astype(BF), emb_ref[...])
    recip = lax.rsqrt(jnp.mean(inputs * inputs, axis=-1, keepdims=True) + EPSILON)
    normed = (inputs * recip * gain_ref[...]).astype(BF)
    place = lax.broadcasted_iota(jnp.int32, (D, 128), 1)
    column = block * 64 + ((place >> 3) << 2) + (place & 3)
    choose = (lax.broadcasted_iota(jnp.int32, (D, 128), 0) == column).astype(F32).astype(BF)
    picked = mm(normed, choose)[:N]
    pick_ref[...] = jnp.concatenate([picked, picked], axis=0).astype(BF)
    row_ref[...] = inputs[N : N + 1]


def pack(rows, width):
    parts = [rows[:, k : k + width] for k in range(0, D, width)]
    if len(parts) * rows.shape[0] < N:
        parts.append(jnp.zeros((N - len(parts) * rows.shape[0], width), F32))
    return jnp.concatenate(parts, axis=0)


def unpack(packed, count, width):
    return jnp.concatenate([packed[k * count : (k + 1) * count] for k in range(D // width)], axis=1)


def share(keys_ref, grads, turn_of, kept_ref, sends):
    unit, ways, count, width = turn_of
    high, low = split(keys_ref[:8, D:] + keys_ref[8:, D:])
    keys_ref[:8, D:] = high
    keys_ref[8:, D:] = low
    place = (lax.axis_index("seq") // unit) % ways
    parts = [grads[k * count : (k + 1) * count] for k in range(ways)]

    def part(index):
        chosen = parts[0]
        for k in range(1, ways):
            chosen = jnp.where(index == k, parts[k], chosen)
        return chosen

    kept_ref[...] = part(place)
    keys = keys_ref[...].astype(BF)
    for k, send_ref in enumerate(sends):
        send_ref[:, :KEYS] = keys
        send_ref[:, KEYS:] = pack(part(place ^ (k + 1)), width).astype(BF)


def first_kernel(got_ref, keys_ref, kept_ref, *sends):
    total = jnp.sum(got_ref[...].astype(F32), axis=0)
    keys_ref[:, :D] = total[:, :D]
    keys_ref[:, D:] = total[:, 2 * D :]
    share(keys_ref, total[:, D : 2 * D], ROUNDS[0], kept_ref, sends)


def key_sum(keys_ref, got, columns):
    return sum((ref[:, columns].astype(F32) for ref in got), keys_ref[:, columns])


def grad_sum(kept_ref, got, turn_of):
    return sum((unpack(ref[:, KEYS:].astype(F32), *turn_of[2:]) for ref in got), kept_ref[...])


def round_kernel(index, old_ref, kept_ref, *refs):
    others = ROUNDS[index][1] - 1
    got, keys_ref, next_ref, sends = refs[:others], refs[others], refs[others + 1], refs[others + 2 :]
    keys_ref[...] = key_sum(old_ref, got, slice(0, KEYS))
    share(keys_ref, grad_sum(kept_ref, got, ROUNDS[index]), ROUNDS[index + 1], next_ref, sends)


def weight_kernel(keys_ref, *refs):
    got, (pick_ref, out_ref) = refs[:-2], refs[-2:]
    both = jnp.concatenate(split(key_sum(keys_ref, got, slice(0, D))), axis=0).astype(BF)
    part = mm_tn(pick_ref[...], both)
    first = (lax.broadcasted_iota(jnp.int32, (128, 512), 0) & 4) == 0
    out_ref[...] = jnp.where(first, part[:, :512], part[:, 512:]).reshape(N, 8, 512).astype(BF)


def row_kernel(keys_ref, kept_ref, *refs):
    got, (row_ref, gain_ref, ge_ref, gg_ref, sums) = refs[:-5], refs[-5:]
    sums[...] = key_sum(keys_ref, got, slice(D, KEYS))
    grad_normed = grad_sum(kept_ref, got, ROUNDS[-1])
    inputs = row_ref[...]
    recip = lax.rsqrt(jnp.mean(inputs * inputs, axis=-1, keepdims=True) + EPSILON)
    grad_scaled = grad_normed * gain_ref[...]
    inner = jnp.mean(grad_scaled * inputs, axis=-1, keepdims=True)
    ge_ref[...] = recip * grad_scaled - inputs * (recip * recip * recip) * inner
    terms = sums[:8] + sums[8:]
    start = (lax.axis_index("seq") * N + lax.axis_index("dp")) * 4
    mine = lax.broadcasted_iota(jnp.int32, (8, 128), 0) == start // 128
    row = jnp.sum(jnp.where(mine, terms, 0.0), axis=0, keepdims=True)
    gg_ref[...] = pltpu.roll(jnp.broadcast_to(row, (8, 128)), 128 - lax.rem(start, 128), 1)


def finish_kernel(got_ref, gk_ref):
    total = jnp.sum(got_ref[...].astype(F32), axis=0)
    gk_ref[:, :512] = total[:4]
    gk_ref[:, 512:] = total[4:]


def call(kernel, outs, ins, scratch=(), flops=0, moved=0, limit=16):
    far_space = pl.BlockSpec(memory_space=pltpu.HBM)
    vmem = pl.BlockSpec(memory_space=pltpu.VMEM)
    return pl.pallas_call(
        kernel,
        out_shape=[jax.ShapeDtypeStruct(shape, kind) for shape, kind in outs],
        in_specs=[far_space if far else vmem for _, far in ins],
        out_specs=[vmem] * len(outs),
        scratch_shapes=list(scratch),
        compiler_params=pltpu.CompilerParams(vmem_limit_bytes=limit * MIB),
        cost_estimate=pl.CostEstimate(flops=flops, bytes_accessed=moved, transcendentals=0),
    )(*[value for value, _ in ins])


def local(byte_ids, embedding, gain, w_query, w_key, w_value, w_out, d_output):
    near_table, base_table = (jnp.asarray(table) for table in angle_tables())
    prev_ids = lax.ppermute(byte_ids, "seq", [(i, i + 1) for i in range(N - 1)])
    gain_row = gain.reshape(1, D)
    mat = pltpu.VMEM((D, D), BF)
    tall = pltpu.VMEM((2 * TOK, D), BF)
    flat = pltpu.VMEM((TOK, D), BF)
    near = lambda *values: [(value, False) for value in values]
    far = lambda *values: [(value, True) for value in values]
    (tables,) = call(
        tables_kernel,
        [((N, N, WIDE), BF)],
        near(prev_ids)
        + far(embedding, near_table, base_table, byte_ids, gain_row)
        + far(w_key, w_value, w_query, d_output[0], w_out),
        [
            pltpu.VMEM((2, 2 * TOK, 128), F32),
            pltpu.VMEM((2, N, 128), F32),
            pltpu.VMEM((1, TOK), jnp.int32),
            pltpu.VMEM((1, D), F32),
            *[flat, mat, mat, mat, flat, mat, tall],
            *[flat] * 8,
            *[tall, tall],
            pltpu.VMEM((VOCAB, D), F32),
            pltpu.VMEM((8, 128), F32),
            pltpu.SemaphoreType.DMA((10,)),
        ],
        flops=8_000_000_000,
        moved=14_000_000,
        limit=56,
    )
    parts = exchange(tables, "dp")
    embedding_later, _ = lax.optimization_barrier((embedding, tables))
    pick, row = call(
        rows_kernel,
        [((32, 128), BF), ((1, D), F32)],
        near(embedding_later, gain_row),
        flops=10_000_000,
        moved=600_000,
    )
    def held(unit, ways, count, width):
        return [((N, KEYS), F32), ((count, D), F32)] + [((N, KEYS + width), BF)] * (ways - 1)

    def spread(sends, unit):
        return [swap(value, unit * (k + 1)) for k, value in enumerate(sends)]

    keys, kept, *sends = call(
        first_kernel, held(*ROUNDS[0]), near(parts), flops=1_000_000, moved=1_300_000
    )
    for index in range(len(ROUNDS) - 1):
        keys, kept, *sends = call(
            functools.partial(round_kernel, index),
            held(*ROUNDS[index + 1]),
            near(keys, kept, *spread(sends, ROUNDS[index][0])),
            flops=1_000_000,
            moved=400_000,
        )
    got = spread(sends, ROUNDS[-1][0])
    (part,) = call(
        weight_kernel, [((N, 8, 512), BF)], near(keys, *got, pick), flops=10_000_000, moved=400_000
    )
    parts = exchange(part, "dp")
    grad_row, gain_own = call(
        row_kernel,
        [((1, D), F32), ((8, 128), F32)],
        near(keys, kept, *got, row, gain_row),
        [pltpu.VMEM((N, 128), F32)],
        flops=1_000_000,
        moved=200_000,
    )
    (grad_weight,) = call(finish_kernel, [((4, D), F32)], near(parts), flops=1_000_000, moved=200_000)
    return grad_weight, gain_own[0, :4], grad_row


def solution(mesh):
    in_specs = (P("dp", "seq"), P(), P(), P(), P(), P(), P(), P("dp", "seq", None))
    out_specs = (P(("seq", "dp"), None), P(("seq", "dp")), P(("seq", "dp"), None))
    return jax.shard_map(local, mesh=mesh, in_specs=in_specs, out_specs=out_specs, check_vma=False)
```

time: 85.1 us -> 82.8 us (0.973)
  blocking collectives: 0 us -> 23.9 us
  waiting for transfers between devices: 36 us -> 14.9 us
  starting transfers between devices: 29.1 us -> 24.5 us
    all_to_all x0 -> x1, blocking collectives: none -> 23.9 us  [exchange(): return lax.all_to_all(value, axis, 0, 0, tiled=False)]
    all_to_all x2 -> x1, waiting for transfers between devices: 25.5 us -> 4.94 us  [exchange(): return lax.all_to_all(value, axis, 0, 0, tiled=False)]
    all_to_all x2 -> x1, starting transfers between devices: 20.7 us -> 7.7 us  [exchange(): return lax.all_to_all(value, axis, 0, 0, tiled=False)]
    ppermute x3 -> x5, starting transfers between devices: 4.06 us -> 12.4 us  [swap(): return lax.ppermute(value, 'seq', [(i, i ^ step) for i in range(N)])]
    ppermute x3 -> x5, waiting for transfers between devices: 9.53 us -> 9.04 us  [swap(): return lax.ppermute(value, 'seq', [(i, i ^ step) for i in range(N)])]
  transfers between devices with their start and end apart: 6 -> 7, of which waited for: 6 -> 6; matrix products, arithmetic and copies ran while one was open for 0% -> 1% of each run, Pallas kernels for 1% -> 1%
where the time goes in v3:
time: 82.8 us; the launch traced here: 82.5 us
  starting transfers between devices  24.5 us (30%)
  blocking collectives  23.9 us (29%)
  Pallas kernels  17.4 us (21%)
  waiting for transfers between devices  14.9 us (18%)
  local copies, waits for them, and re-layouts  1.08 us (1%)
    all_to_all x1, blocking collectives, exchange(): return lax.all_to_all(value, axis, 0, 0, tiled=False)  23.9 us
    pallas_call x8, Pallas kernels, call(): pl.pallas_call(kernel, out_shape=[jax.ShapeDtypeStruct(shape, kind) for s...  17.4 us
    ppermute x5, starting transfers between devices, swap(): return lax.ppermute(value, 'seq', [(i, i ^ step) for i in range(N)])  12.4 us
    ppermute x5, waiting for transfers between devices, swap(): return lax.ppermute(value, 'seq', [(i, i ^ step) for i in range(N)])  9.04 us
    all_to_all x1, starting transfers between devices, exchange(): return lax.all_to_all(value, axis, 0, 0, tiled=False)  7.7 us
    all_to_all x1, waiting for transfers between devices, exchange(): return lax.all_to_all(value, axis, 0, 0, tiled=False)  4.94 us
    ppermute x1, starting transfers between devices, local(): prev_ids = lax.ppermute(byte_ids, 'seq', [(i, i + 1) for i in range(N - 1)])  4.37 us
  transfers between devices with their start and end apart: 7, of which 6 were waited for; matrix products, arithmetic and copies ran while one was open for 1% of the time, Pallas kernels for 1%

profile of v3, /device:TPU:1, one launch (start us, length us, event | category | flops | bytes accessed | tf_op | source)
XLA Modules:
  0.0 82.5 jit_solution(1917835498254130327)
XLA Ops:
  0.6 4.4 %collective-permute-start = (s32[1,256]{1,0:T(1,128)}, s32[1,256]{1,0:T(1,128)S(1)}, u32[]{:S(2)}, u32[]{:S(2)}) collective-permute-start(s32[1,256]{1,0:T(1,128)} %refs_4_.1), channel_id=1, source_target_pairs={{0,16},{16,32},{32,48},{48,64},{64,80},{80,96},{96,112},{112,128},... | collective-permute-start | bytes 3080 | tf_op jit(solution)/shard_map/ppermute | solution.py:312
  5.0 0.9 %collective-permute-done.refs_0_ = s32[1,256]{1,0:T(1,128)S(1)} collective-permute-done((s32[1,256]{1,0:T(1,128)}, s32[1,256]{1,0:T(1,128)S(1)}, u32[]{:S(2)}, u32[]{:S(2)}) %collective-permute-start) | collective-permute-done | bytes 1056 | tf_op jit(solution)/shard_map/ppermute | solution.py:312
  5.9 0.0 copy-start.2
  5.9 0.6 copy-done.2
  6.5 14.5 %shard_map.121 = bf16[16,16,2176]{2,1,0:T(8,128)(2,1)} custom-call(s32[1,256]{1,0:T(1,128)} %copy-done.2, bf16[256,1024]{1,0:T(8,128)(2,1)} %emb_ref, f32[2,512,128]{2,1,0:T(8,128)} %constant.4.clone.refs_2_, f32[2,16,128]{2,1,0:T(8,128)} %constant.5.clone.refs_3_, s32[1,256]{1,0:T(1,128)} %refs_4_.1, f32[1,1024]{1,0:T(1,128)} %bitcast.4, ...), custom_call_target="tpu_custom_call" | custom-call | flops 8000000000 | bytes 14000000 | tf_op jit(solution)/shard_map/pallas_call | solution.py:299
  21.0 0.0 copy-start
  21.0 0.0 copy-start.1
  21.0 23.9 %all_to_all.10.got_ref = bf16[16,16,2176]{2,1,0:T(8,128)(2,1)S(1)} all-to-all(bf16[16,16,2176]{2,1,0:T(8,128)(2,1)} %shard_map.121), channel_id=1, replica_groups=mesh['seq'=16,'dp'=16] {'dp'}, dimensions={0} | all-to-all | bytes 2228224 | tf_op jit(solution)/shard_map/all_to_all | solution.py:30
  44.9 0.2 shard_map.122
  45.1 2.1 %collective-permute-start.1 = (bf16[16,1408]{1,0:T(8,128)(2,1)S(1)}, bf16[16,1408]{1,0:T(8,128)(2,1)S(1)}, u32[]{:S(2)}, u32[]{:S(2)}) collective-permute-start(bf16[16,1408]{1,0:T(8,128)(2,1)S(1)} %get-tuple-element.21), channel_id=1, source_target_pairs={{0,16},{16,0},{32,48},{48,32},{64,80},{80,64},{96,112},{112,96},{1... | collective-permute-start | bytes 135176 | tf_op jit(solution)/shard_map/ppermute | solution.py:34
  47.2 3.8 %collective-permute-start.2 = (bf16[16,1408]{1,0:T(8,128)(2,1)S(1)}, bf16[16,1408]{1,0:T(8,128)(2,1)S(1)}, u32[]{:S(2)}, u32[]{:S(2)}) collective-permute-start(bf16[16,1408]{1,0:T(8,128)(2,1)S(1)} %get-tuple-element.22), channel_id=1, source_target_pairs={{0,32},{16,48},{32,0},{48,16},{64,96},{80,112},{96,64},{112,80},{1... | collective-permute-start | bytes 135176 | tf_op jit(solution)/shard_map/ppermute | solution.py:34
  51.0 0.1 collective-permute-start.3
  51.1 0.0 collective-permute-done.1.refs_0_
  51.1 1.6 %collective-permute-done.2.refs_1_ = bf16[16,1408]{1,0:T(8,128)(2,1)S(1)} collective-permute-done((bf16[16,1408]{1,0:T(8,128)(2,1)S(1)}, bf16[16,1408]{1,0:T(8,128)(2,1)S(1)}, u32[]{:S(2)}, u32[]{:S(2)}) %collective-permute-start.2) | collective-permute-done | bytes 45088 | tf_op jit(solution)/shard_map/ppermute | solution.py:34
  52.8 3.0 %collective-permute-done.3.refs_2_ = bf16[16,1408]{1,0:T(8,128)(2,1)S(1)} collective-permute-done((bf16[16,1408]{1,0:T(8,128)(2,1)S(1)}, bf16[16,1408]{1,0:T(8,128)(2,1)S(1)}, u32[]{:S(2)}, u32[]{:S(2)}) %collective-permute-start.3) | collective-permute-done | bytes 45088 | tf_op jit(solution)/shard_map/ppermute | solution.py:34
  55.8 2.8 %collective-permute-start.4 = (bf16[16,1280]{1,0:T(8,128)(2,1)S(1)}, bf16[16,1280]{1,0:T(8,128)(2,1)S(1)}, u32[]{:S(2)}, u32[]{:S(2)}) collective-permute-start(bf16[16,1280]{1,0:T(8,128)(2,1)S(1)} %get-tuple-element.26), channel_id=1, source_target_pairs={{0,128},{16,144},{32,160},{48,176},{64,192},{80,208},{96,224},{112... | collective-permute-start | bytes 122888 | tf_op jit(solution)/shard_map/ppermute | solution.py:34
  58.6 1.6 %collective-permute-done.4.refs_0_ = bf16[16,1280]{1,0:T(8,128)(2,1)S(1)} collective-permute-done((bf16[16,1280]{1,0:T(8,128)(2,1)S(1)}, bf16[16,1280]{1,0:T(8,128)(2,1)S(1)}, u32[]{:S(2)}, u32[]{:S(2)}) %collective-permute-start.4) | collective-permute-done | bytes 40992 | tf_op jit(solution)/shard_map/ppermute | solution.py:34
  60.2 3.6 %collective-permute-start.5 = (bf16[16,1280]{1,0:T(8,128)(2,1)S(1)}, bf16[16,1280]{1,0:T(8,128)(2,1)S(1)}, u32[]{:S(2)}, u32[]{:S(2)}) collective-permute-start(bf16[16,1280]{1,0:T(8,128)(2,1)S(1)} %get-tuple-element.28), channel_id=1, source_target_pairs={{0,64},{16,80},{32,96},{48,112},{64,0},{80,16},{96,32},{112,48},{1... | collective-permute-start | bytes 122888 | tf_op jit(solution)/shard_map/ppermute | solution.py:34
  63.8 0.0 copy-done
  63.8 0.0 copy-done.1
  63.8 0.4 shard_map.125
  64.3 2.8 %collective-permute-done.5.refs_0_ = bf16[16,1280]{1,0:T(8,128)(2,1)S(1)} collective-permute-done((bf16[16,1280]{1,0:T(8,128)(2,1)S(1)}, bf16[16,1280]{1,0:T(8,128)(2,1)S(1)}, u32[]{:S(2)}, u32[]{:S(2)}) %collective-permute-start.5) | collective-permute-done | bytes 40992 | tf_op jit(solution)/shard_map/ppermute | solution.py:34
  67.1 0.9 %shard_map.126 = bf16[16,8,512]{2,1,0:T(8,128)(2,1)} custom-call(f32[16,1152]{1,0:T(8,128)S(1)} %get-tuple-element.27.keys_ref, bf16[16,1280]{1,0:T(8,128)(2,1)S(1)} %collective-permute-done.5.refs_0_, bf16[32,128]{1,0:T(8,128)(2,1)S(1)} %get-tuple-element.30.refs_1_), custom_call_target="tpu_custom_call" | custom-call | flops 10000000 | bytes 400000 | tf_op jit(solution)/shard_map/pallas_call | solution.py:299
  68.0 7.7 %all-to-all-start.1 = ((bf16[16,8,512]{2,1,0:T(8,128)(2,1)}), bf16[16,8,512]{2,1,0:T(8,128)(2,1)S(1)}, u32[]{:S(2)}, u32[]{:S(2)}) async-start(bf16[16,8,512]{2,1,0:T(8,128)(2,1)} %shard_map.126), calls=%async_computation.1 | async-start | bytes 262144 | tf_op jit(solution)/shard_map/all_to_all | solution.py:30
  75.7 0.7 shard_map.128
  76.4 0.5 slice_bitcast_fusion
  76.9 4.9 %all-to-all-done.1.got_ref = bf16[16,8,512]{2,1,0:T(8,128)(2,1)S(1)} async-done(((bf16[16,8,512]{2,1,0:T(8,128)(2,1)}), bf16[16,8,512]{2,1,0:T(8,128)(2,1)S(1)}, u32[]{:S(2)}, u32[]{:S(2)}) %all-to-all-start.1) | async-done | bytes 131104 | tf_op jit(solution)/shard_map/all_to_all | solution.py:30
  81.9 0.6 shard_map.127
  (2 shorter events, 0.1 us)
Async XLA Ops:
  0.6 5.3 %collective-permute-start = (s32[1,256]{1,0:T(1,128)}, s32[1,256]{1,0:T(1,128)S(1)}, u32[]{:S(2)}, u32[]{:S(2)}) collective-permute-start(s32[1,256]{1,0:T(1,128)} %refs_4_.1), channel_id=1, source_target_pairs={{0,16},{16,32},{32,48},{48,64},{64,80},{80,96},{96,112},{112,128},... | collective-permute-start | bytes 3080 | tf_op jit(solution)/shard_map/ppermute | solution.py:312
  5.9 0.6 copy-start.2
  21.0 42.8 %copy-start = (bf16[256,1024]{1,0:T(8,128)(2,1)S(1)}, bf16[256,1024]{1,0:T(8,128)(2,1)}, u32[]{:S(2)}) copy-start(bf16[256,1024]{1,0:T(8,128)(2,1)} %emb_ref) | copy-start | bytes 1572868
  21.0 42.8 %copy-start.1 = (f32[1024]{0:T(1024)S(1)}, f32[1024]{0:T(1024)}, u32[]{:S(2)}) copy-start(f32[1024]{0:T(1024)} %param.12) | copy-start | bytes 12292
  45.1 6.0 %collective-permute-start.1 = (bf16[16,1408]{1,0:T(8,128)(2,1)S(1)}, bf16[16,1408]{1,0:T(8,128)(2,1)S(1)}, u32[]{:S(2)}, u32[]{:S(2)}) collective-permute-start(bf16[16,1408]{1,0:T(8,128)(2,1)S(1)} %get-tuple-element.21), channel_id=1, source_target_pairs={{0,16},{16,0},{32,48},{48,32},{64,80},{80,64},{96,112},{112,96},{1... | collective-permute-start | bytes 135176 | tf_op jit(solution)/shard_map/ppermute | solution.py:34
  47.2 5.6 %collective-permute-start.2 = (bf16[16,1408]{1,0:T(8,128)(2,1)S(1)}, bf16[16,1408]{1,0:T(8,128)(2,1)S(1)}, u32[]{:S(2)}, u32[]{:S(2)}) collective-permute-start(bf16[16,1408]{1,0:T(8,128)(2,1)S(1)} %get-tuple-element.22), channel_id=1, source_target_pairs={{0,32},{16,48},{32,0},{48,16},{64,96},{80,112},{96,64},{112,80},{1... | collective-permute-start | bytes 135176 | tf_op jit(solution)/shard_map/ppermute | solution.py:34
  51.0 4.7 %collective-permute-start.3 = (bf16[16,1408]{1,0:T(8,128)(2,1)S(1)}, bf16[16,1408]{1,0:T(8,128)(2,1)S(1)}, u32[]{:S(2)}, u32[]{:S(2)}) collective-permute-start(bf16[16,1408]{1,0:T(8,128)(2,1)S(1)} %get-tuple-element.23), channel_id=1, source_target_pairs={{0,48},{16,32},{32,16},{48,0},{64,112},{80,96},{96,80},{112,64},{1... | collective-permute-start | bytes 135176 | tf_op jit(solution)/shard_map/ppermute | solution.py:34
  55.8 4.4 %collective-permute-start.4 = (bf16[16,1280]{1,0:T(8,128)(2,1)S(1)}, bf16[16,1280]{1,0:T(8,128)(2,1)S(1)}, u32[]{:S(2)}, u32[]{:S(2)}) collective-permute-start(bf16[16,1280]{1,0:T(8,128)(2,1)S(1)} %get-tuple-element.26), channel_id=1, source_target_pairs={{0,128},{16,144},{32,160},{48,176},{64,192},{80,208},{96,224},{112... | collective-permute-start | bytes 122888 | tf_op jit(solution)/shard_map/ppermute | solution.py:34
  60.2 6.8 %collective-permute-start.5 = (bf16[16,1280]{1,0:T(8,128)(2,1)S(1)}, bf16[16,1280]{1,0:T(8,128)(2,1)S(1)}, u32[]{:S(2)}, u32[]{:S(2)}) collective-permute-start(bf16[16,1280]{1,0:T(8,128)(2,1)S(1)} %get-tuple-element.28), channel_id=1, source_target_pairs={{0,64},{16,80},{32,96},{48,112},{64,0},{80,16},{96,32},{112,48},{1... | collective-permute-start | bytes 122888 | tf_op jit(solution)/shard_map/ppermute | solution.py:34
  68.0 13.9 %all-to-all-start.1 = ((bf16[16,8,512]{2,1,0:T(8,128)(2,1)}), bf16[16,8,512]{2,1,0:T(8,128)(2,1)S(1)}, u32[]{:S(2)}, u32[]{:S(2)}) async-start(bf16[16,8,512]{2,1,0:T(8,128)(2,1)} %shard_map.126), calls=%async_computation.1 | async-start | bytes 262144 | tf_op jit(solution)/shard_map/all_to_all | solution.py:30

commit v4 on v3

--- a/solution.py
+++ b/solution.py
@@ -105,27 +105,32 @@
 
 
 def tables_kernel(*refs):
-    prev_ref, sources, (out_ref,) = refs[0], refs[1:11], refs[11:12]
-    near_ref, base_ref, ids_ref, gain_ref, emb, wk, wv, wq, do, wo = refs[12:22]
-    tab, q_ref, k_ref, v_ref, ga_ref, kprev, vprev, vtab, gq, kg, vg, scaled, terms, sems = refs[22:]
-    kept = (emb, near_ref, base_ref, ids_ref, gain_ref, wk, wv, wq, do, wo)
+    sources, (out_ref,) = refs[:11], refs[11:12]
+    prev_ref, near_ref, base_ref, ids_ref, gain_ref, emb, wk, wv, wq, do, wo = refs[12:23]
+    tab, q_ref, k_ref, v_ref, ga_ref, kprev, vprev, vtab, gq, kg, vg, scaled, terms, sems = refs[23:]
+    kept = (emb, gain_ref, ids_ref, prev_ref, near_ref, base_ref, wk, wv, wq, do, wo)
     copies = [pltpu.make_async_copy(s, d, sems.at[i]) for i, (s, d) in enumerate(zip(sources, kept))]
-    for copy in copies:
+    for copy in copies[:7]:
         copy.start()
     block = lax.axis_index("seq")
     place = lax.broadcasted_iota(jnp.int32, (VOCAB, VOCAB), 0)
     value = lax.broadcasted_iota(jnp.int32, (VOCAB, VOCAB), 1)
     order = (table_row(value) == place).astype(F32).astype(BF)
-    for copy in copies[:5]:
+    copies[0].wait()
+    copies[1].wait()
+    copies[7].start()
+    copies[8].start()
+    inputs = mm(order, emb[...])
+    recip = lax.rsqrt(jnp.mean(inputs * inputs, axis=-1, keepdims=True) + EPSILON)
+    scaled[...] = inputs * recip
+    normed = (scaled[...] * gain_ref[...]).astype(BF)
+
+    for copy in copies[2:6]:
         copy.wait()
     hot_own, hot_prev = hot_columns(ids_ref[...]), hot_columns(prev_ref[...])
     rows_own, rows_prev = hot_own.T, hot_prev.T
     cos_p, sin_p = turn_tables(near_ref, base_ref, slice(0, TOK), block)
     cos_o, sin_o = turn_tables(near_ref, base_ref, slice(TOK, 2 * TOK), block)
-    inputs = mm(order, emb[...])
-    recip = lax.rsqrt(jnp.mean(inputs * inputs, axis=-1, keepdims=True) + EPSILON)
-    scaled[...] = inputs * recip
-    normed = (scaled[...] * gain_ref[...]).astype(BF)
 
     def fill(weight):
         full = mm(normed, weight[...])
@@ -138,19 +143,21 @@
         for h in range(HEADS):
             out_ref[:, head(h)] = turn(full[:, head(h)], cosine, sine).astype(BF)
 
-    copies[5].wait()
+    copies[6].wait()
+    copies[9].start()
+    copies[10].start()
     fill(wk)
     gather(rows_own, cos_o, sin_o, k_ref)
     gather(rows_prev, cos_p, sin_p, kprev)
-    copies[6].wait()
+    copies[7].wait()
     vtab[...] = mm(normed, wv[...]).astype(BF)
     v_ref[...] = mm(rows_own, vtab[...]).astype(BF)
     vprev[...] = mm(rows_prev, vtab[...]).astype(BF)
-    copies[7].wait()
+    copies[8].wait()
     fill(wq)
     gather(rows_own, cos_o, sin_o, q_ref)
-    copies[8].wait()
     copies[9].wait()
+    copies[10].wait()
     ga_ref[...] = mm(do[...], wo[...]).astype(BF)
     lead = jnp.where(block == 0, NEGATIVE, 0.0).astype(F32)
     scale = HEAD_DIM ** (-0.5)
@@ -294,7 +301,7 @@
 
 
 def call(kernel, outs, ins, scratch=(), flops=0, moved=0, limit=16):
-    far_space = pl.BlockSpec(memory_space=pltpu.HBM)
+    far_space = pl.BlockSpec(memory_space=pl.ANY)
     vmem = pl.BlockSpec(memory_space=pltpu.VMEM)
     return pl.pallas_call(
         kernel,
@@ -319,10 +326,10 @@
     (tables,) = call(
         tables_kernel,
         [((N, N, WIDE), BF)],
-        near(prev_ids)
-        + far(embedding, near_table, base_table, byte_ids, gain_row)
+        far(embedding, gain_row, byte_ids, prev_ids, near_table, base_table)
         + far(w_key, w_value, w_query, d_output[0], w_out),
         [
+            pltpu.VMEM((1, TOK), jnp.int32),
             pltpu.VMEM((2, 2 * TOK, 128), F32),
             pltpu.VMEM((2, N, 128), F32),
             pltpu.VMEM((1, TOK), jnp.int32),
@@ -332,7 +339,7 @@
             *[tall, tall],
             pltpu.VMEM((VOCAB, D), F32),
             pltpu.VMEM((8, 128), F32),
-            pltpu.SemaphoreType.DMA((10,)),
+            pltpu.SemaphoreType.DMA((11,)),
         ],
         flops=8_000_000_000,
         moved=14_000_000,

time: 82.8 us -> 82.1 us (level)
  no operation moved by 1% of the time
where the time goes in v4:
time: 82.1 us; the launch traced here: 81.8 us
  starting transfers between devices  24.5 us (30%)
  blocking collectives  23.9 us (29%)
  Pallas kernels  16.8 us (20%)
  waiting for transfers between devices  14.9 us (18%)
  local copies, waits for them, and re-layouts  1.08 us (1%)
    all_to_all x1, blocking collectives, exchange(): return lax.all_to_all(value, axis, 0, 0, tiled=False)  23.9 us
    pallas_call x8, Pallas kernels, call(): pl.pallas_call(kernel, out_shape=[jax.ShapeDtypeStruct(shape, kind) for s...  16.8 us
    ppermute x5, starting transfers between devices, swap(): return lax.ppermute(value, 'seq', [(i, i ^ step) for i in range(N)])  12.4 us
    ppermute x5, waiting for transfers between devices, swap(): return lax.ppermute(value, 'seq', [(i, i ^ step) for i in range(N)])  9.05 us
    all_to_all x1, starting transfers between devices, exchange(): return lax.all_to_all(value, axis, 0, 0, tiled=False)  7.7 us
    all_to_all x1, waiting for transfers between devices, exchange(): return lax.all_to_all(value, axis, 0, 0, tiled=False)  4.94 us
    ppermute x1, starting transfers between devices, local(): prev_ids = lax.ppermute(byte_ids, 'seq', [(i, i + 1) for i in range(N - 1)])  4.37 us
  transfers between devices with their start and end apart: 7, of which 6 were waited for; matrix products, arithmetic and copies ran while one was open for 1% of the time, Pallas kernels for 1%

profile of v4, /device:TPU:1, one launch (start us, length us, event | category | flops | bytes accessed | tf_op | source)
XLA Modules:
  0.0 81.8 jit_solution(9350384972192304246)
XLA Ops:
  0.6 4.4 %collective-permute-start = (s32[1,256]{1,0:T(1,128)}, s32[1,256]{1,0:T(1,128)S(1)}, u32[]{:S(2)}, u32[]{:S(2)}) collective-permute-start(s32[1,256]{1,0:T(1,128)} %refs_2_.1), channel_id=1, source_target_pairs={{0,16},{16,32},{32,48},{48,64},{64,80},{80,96},{96,112},{112,128},... | collective-permute-start | bytes 3080 | tf_op jit(solution)/shard_map/ppermute | solution.py:319
  5.0 0.9 %collective-permute-done.refs_3_ = s32[1,256]{1,0:T(1,128)S(1)} collective-permute-done((s32[1,256]{1,0:T(1,128)}, s32[1,256]{1,0:T(1,128)S(1)}, u32[]{:S(2)}, u32[]{:S(2)}) %collective-permute-start) | collective-permute-done | bytes 1056 | tf_op jit(solution)/shard_map/ppermute | solution.py:319
  5.9 0.0 copy-start.2
  5.9 0.6 copy-done.2
  6.5 13.8 %shard_map.121 = bf16[16,16,2176]{2,1,0:T(8,128)(2,1)} custom-call(bf16[256,1024]{1,0:T(8,128)(2,1)} %emb_ref, f32[1,1024]{1,0:T(1,128)} %bitcast.4, s32[1,256]{1,0:T(1,128)} %refs_2_.1, s32[1,256]{1,0:T(1,128)} %copy-done.2, f32[2,512,128]{2,1,0:T(8,128)} %constant.4.clone.refs_4_, f32[2,16,128]{2,1,0:T(8,128)} %constant.5.clone.refs_5_, ...), custom_call_target="tpu_custom_call" | custom-call | flops 8000000000 | bytes 14000000 | tf_op jit(solution)/shard_map/pallas_call | solution.py:306
  20.3 0.0 copy-start
  20.3 0.0 copy-start.1
  20.3 23.9 %all_to_all.10.got_ref = bf16[16,16,2176]{2,1,0:T(8,128)(2,1)S(1)} all-to-all(bf16[16,16,2176]{2,1,0:T(8,128)(2,1)} %shard_map.121), channel_id=1, replica_groups=mesh['seq'=16,'dp'=16] {'dp'}, dimensions={0} | all-to-all | bytes 2228224 | tf_op jit(solution)/shard_map/all_to_all | solution.py:30
  44.2 0.2 shard_map.122
  44.4 2.1 %collective-permute-start.1 = (bf16[16,1408]{1,0:T(8,128)(2,1)S(1)}, bf16[16,1408]{1,0:T(8,128)(2,1)S(1)}, u32[]{:S(2)}, u32[]{:S(2)}) collective-permute-start(bf16[16,1408]{1,0:T(8,128)(2,1)S(1)} %get-tuple-element.21), channel_id=1, source_target_pairs={{0,16},{16,0},{32,48},{48,32},{64,80},{80,64},{96,112},{112,96},{1... | collective-permute-start | bytes 135176 | tf_op jit(solution)/shard_map/ppermute | solution.py:34
  46.5 3.9 %collective-permute-start.2 = (bf16[16,1408]{1,0:T(8,128)(2,1)S(1)}, bf16[16,1408]{1,0:T(8,128)(2,1)S(1)}, u32[]{:S(2)}, u32[]{:S(2)}) collective-permute-start(bf16[16,1408]{1,0:T(8,128)(2,1)S(1)} %get-tuple-element.22), channel_id=1, source_target_pairs={{0,32},{16,48},{32,0},{48,16},{64,96},{80,112},{96,64},{112,80},{1... | collective-permute-start | bytes 135176 | tf_op jit(solution)/shard_map/ppermute | solution.py:34
  50.4 0.1 collective-permute-start.3
  50.5 0.0 collective-permute-done.1.refs_0_
  50.5 1.6 %collective-permute-done.2.refs_1_ = bf16[16,1408]{1,0:T(8,128)(2,1)S(1)} collective-permute-done((bf16[16,1408]{1,0:T(8,128)(2,1)S(1)}, bf16[16,1408]{1,0:T(8,128)(2,1)S(1)}, u32[]{:S(2)}, u32[]{:S(2)}) %collective-permute-start.2) | collective-permute-done | bytes 45088 | tf_op jit(solution)/shard_map/ppermute | solution.py:34
  52.1 3.0 %collective-permute-done.3.refs_2_ = bf16[16,1408]{1,0:T(8,128)(2,1)S(1)} collective-permute-done((bf16[16,1408]{1,0:T(8,128)(2,1)S(1)}, bf16[16,1408]{1,0:T(8,128)(2,1)S(1)}, u32[]{:S(2)}, u32[]{:S(2)}) %collective-permute-start.3) | collective-permute-done | bytes 45088 | tf_op jit(solution)/shard_map/ppermute | solution.py:34
  55.1 2.8 %collective-permute-start.4 = (bf16[16,1280]{1,0:T(8,128)(2,1)S(1)}, bf16[16,1280]{1,0:T(8,128)(2,1)S(1)}, u32[]{:S(2)}, u32[]{:S(2)}) collective-permute-start(bf16[16,1280]{1,0:T(8,128)(2,1)S(1)} %get-tuple-element.26), channel_id=1, source_target_pairs={{0,128},{16,144},{32,160},{48,176},{64,192},{80,208},{96,224},{112... | collective-permute-start | bytes 122888 | tf_op jit(solution)/shard_map/ppermute | solution.py:34
  57.9 1.6 %collective-permute-done.4.refs_0_ = bf16[16,1280]{1,0:T(8,128)(2,1)S(1)} collective-permute-done((bf16[16,1280]{1,0:T(8,128)(2,1)S(1)}, bf16[16,1280]{1,0:T(8,128)(2,1)S(1)}, u32[]{:S(2)}, u32[]{:S(2)}) %collective-permute-start.4) | collective-permute-done | bytes 40992 | tf_op jit(solution)/shard_map/ppermute | solution.py:34
  59.6 3.6 %collective-permute-start.5 = (bf16[16,1280]{1,0:T(8,128)(2,1)S(1)}, bf16[16,1280]{1,0:T(8,128)(2,1)S(1)}, u32[]{:S(2)}, u32[]{:S(2)}) collective-permute-start(bf16[16,1280]{1,0:T(8,128)(2,1)S(1)} %get-tuple-element.28), channel_id=1, source_target_pairs={{0,64},{16,80},{32,96},{48,112},{64,0},{80,16},{96,32},{112,48},{1... | collective-permute-start | bytes 122888 | tf_op jit(solution)/shard_map/ppermute | solution.py:34
  63.2 0.0 copy-done
  63.2 0.0 copy-done.1
  63.2 0.4 shard_map.125
  63.6 2.8 %collective-permute-done.5.refs_0_ = bf16[16,1280]{1,0:T(8,128)(2,1)S(1)} collective-permute-done((bf16[16,1280]{1,0:T(8,128)(2,1)S(1)}, bf16[16,1280]{1,0:T(8,128)(2,1)S(1)}, u32[]{:S(2)}, u32[]{:S(2)}) %collective-permute-start.5) | collective-permute-done | bytes 40992 | tf_op jit(solution)/shard_map/ppermute | solution.py:34
  66.4 0.9 %shard_map.126 = bf16[16,8,512]{2,1,0:T(8,128)(2,1)} custom-call(f32[16,1152]{1,0:T(8,128)S(1)} %get-tuple-element.27.keys_ref, bf16[16,1280]{1,0:T(8,128)(2,1)S(1)} %collective-permute-done.5.refs_0_, bf16[32,128]{1,0:T(8,128)(2,1)S(1)} %get-tuple-element.30.refs_1_), custom_call_target="tpu_custom_call" | custom-call | flops 10000000 | bytes 400000 | tf_op jit(solution)/shard_map/pallas_call | solution.py:306
  67.3 7.7 %all-to-all-start.1 = ((bf16[16,8,512]{2,1,0:T(8,128)(2,1)}), bf16[16,8,512]{2,1,0:T(8,128)(2,1)S(1)}, u32[]{:S(2)}, u32[]{:S(2)}) async-start(bf16[16,8,512]{2,1,0:T(8,128)(2,1)} %shard_map.126), calls=%async_computation.1 | async-start | bytes 262144 | tf_op jit(solution)/shard_map/all_to_all | solution.py:30
  75.0 0.7 shard_map.128
  75.7 0.5 slice_bitcast_fusion
  76.3 4.9 %all-to-all-done.1.got_ref = bf16[16,8,512]{2,1,0:T(8,128)(2,1)S(1)} async-done(((bf16[16,8,512]{2,1,0:T(8,128)(2,1)}), bf16[16,8,512]{2,1,0:T(8,128)(2,1)S(1)}, u32[]{:S(2)}, u32[]{:S(2)}) %all-to-all-start.1) | async-done | bytes 131104 | tf_op jit(solution)/shard_map/all_to_all | solution.py:30
  81.2 0.6 shard_map.127
  (2 shorter events, 0.1 us)
Async XLA Ops:
  0.6 5.3 %collective-permute-start = (s32[1,256]{1,0:T(1,128)}, s32[1,256]{1,0:T(1,128)S(1)}, u32[]{:S(2)}, u32[]{:S(2)}) collective-permute-start(s32[1,256]{1,0:T(1,128)} %refs_2_.1), channel_id=1, source_target_pairs={{0,16},{16,32},{32,48},{48,64},{64,80},{80,96},{96,112},{112,128},... | collective-permute-start | bytes 3080 | tf_op jit(solution)/shard_map/ppermute | solution.py:319
  5.9 0.6 copy-start.2
  20.3 42.9 %copy-start = (bf16[256,1024]{1,0:T(8,128)(2,1)S(1)}, bf16[256,1024]{1,0:T(8,128)(2,1)}, u32[]{:S(2)}) copy-start(bf16[256,1024]{1,0:T(8,128)(2,1)} %emb_ref) | copy-start | bytes 1572868
  20.3 42.8 %copy-start.1 = (f32[1024]{0:T(1024)S(1)}, f32[1024]{0:T(1024)}, u32[]{:S(2)}) copy-start(f32[1024]{0:T(1024)} %param.12) | copy-start | bytes 12292
  44.4 6.0 %collective-permute-start.1 = (bf16[16,1408]{1,0:T(8,128)(2,1)S(1)}, bf16[16,1408]{1,0:T(8,128)(2,1)S(1)}, u32[]{:S(2)}, u32[]{:S(2)}) collective-permute-start(bf16[16,1408]{1,0:T(8,128)(2,1)S(1)} %get-tuple-element.21), channel_id=1, source_target_pairs={{0,16},{16,0},{32,48},{48,32},{64,80},{80,64},{96,112},{112,96},{1... | collective-permute-start | bytes 135176 | tf_op jit(solution)/shard_map/ppermute | solution.py:34
  46.5 5.6 %collective-permute-start.2 = (bf16[16,1408]{1,0:T(8,128)(2,1)S(1)}, bf16[16,1408]{1,0:T(8,128)(2,1)S(1)}, u32[]{:S(2)}, u32[]{:S(2)}) collective-permute-start(bf16[16,1408]{1,0:T(8,128)(2,1)S(1)} %get-tuple-element.22), channel_id=1, source_target_pairs={{0,32},{16,48},{32,0},{48,16},{64,96},{80,112},{96,64},{112,80},{1... | collective-permute-start | bytes 135176 | tf_op jit(solution)/shard_map/ppermute | solution.py:34
  50.4 4.7 %collective-permute-start.3 = (bf16[16,1408]{1,0:T(8,128)(2,1)S(1)}, bf16[16,1408]{1,0:T(8,128)(2,1)S(1)}, u32[]{:S(2)}, u32[]{:S(2)}) collective-permute-start(bf16[16,1408]{1,0:T(8,128)(2,1)S(1)} %get-tuple-element.23), channel_id=1, source_target_pairs={{0,48},{16,32},{32,16},{48,0},{64,112},{80,96},{96,80},{112,64},{1... | collective-permute-start | bytes 135176 | tf_op jit(solution)/shard_map/ppermute | solution.py:34
  55.1 4.4 %collective-permute-start.4 = (bf16[16,1280]{1,0:T(8,128)(2,1)S(1)}, bf16[16,1280]{1,0:T(8,128)(2,1)S(1)}, u32[]{:S(2)}, u32[]{:S(2)}) collective-permute-start(bf16[16,1280]{1,0:T(8,128)(2,1)S(1)} %get-tuple-element.26), channel_id=1, source_target_pairs={{0,128},{16,144},{32,160},{48,176},{64,192},{80,208},{96,224},{112... | collective-permute-start | bytes 122888 | tf_op jit(solution)/shard_map/ppermute | solution.py:34
  59.6 6.8 %collective-permute-start.5 = (bf16[16,1280]{1,0:T(8,128)(2,1)S(1)}, bf16[16,1280]{1,0:T(8,128)(2,1)S(1)}, u32[]{:S(2)}, u32[]{:S(2)}) collective-permute-start(bf16[16,1280]{1,0:T(8,128)(2,1)S(1)} %get-tuple-element.28), channel_id=1, source_target_pairs={{0,64},{16,80},{32,96},{48,112},{64,0},{80,16},{96,32},{112,48},{1... | collective-permute-start | bytes 122888 | tf_op jit(solution)/shard_map/ppermute | solution.py:34
  67.3 13.9 %all-to-all-start.1 = ((bf16[16,8,512]{2,1,0:T(8,128)(2,1)}), bf16[16,8,512]{2,1,0:T(8,128)(2,1)S(1)}, u32[]{:S(2)}, u32[]{:S(2)}) async-start(bf16[16,8,512]{2,1,0:T(8,128)(2,1)} %shard_map.126), calls=%async_computation.1 | async-start | bytes 262144 | tf_op jit(solution)/shard_map/all_to_all | solution.py:30

commit v5 on v4

--- a/solution.py
+++ b/solution.py
@@ -105,9 +105,9 @@
 
 
 def tables_kernel(*refs):
-    sources, (out_ref,) = refs[:11], refs[11:12]
+    sources, result_ref = refs[:11], refs[11]
     prev_ref, near_ref, base_ref, ids_ref, gain_ref, emb, wk, wv, wq, do, wo = refs[12:23]
-    tab, q_ref, k_ref, v_ref, ga_ref, kprev, vprev, vtab, gq, kg, vg, scaled, terms, sems = refs[23:]
+    tab, q_ref, k_ref, v_ref, ga_ref, kprev, vprev, vtab, gq, kg, vg, scaled, terms, out_ref, sems = refs[23:]
     kept = (emb, gain_ref, ids_ref, prev_ref, near_ref, base_ref, wk, wv, wq, do, wo)
     copies = [pltpu.make_async_copy(s, d, sems.at[i]) for i, (s, d) in enumerate(zip(sources, kept))]
     for copy in copies[:7]:
@@ -191,6 +191,12 @@
     hot2 = jnp.concatenate([hot_prev, hot_own], axis=1)
     key_table = mm(hot2, kg[...]).astype(BF)
     out_ref[:, :, :D] = key_table.reshape(N, N, D)
+    parts = [slice(0, D), slice(D, WIDE)]
+    leaving = [
+        pltpu.make_async_copy(out_ref.at[:, :, part], result_ref.at[:, :, part], sems.at[11 + i])
+        for i, part in enumerate(parts)
+    ]
+    leaving[0].start()
     value_table = mm(hot2, vg[...]).astype(BF)
     query_table = mm(hot_own, gq[...]).astype(BF)
     grad_normed = mm_nt(key_table, wk[...]) + mm_nt(value_table, wv[...]) + mm_nt(query_table, wq[...])
@@ -198,6 +204,9 @@
     product = jnp.sum(grad_normed * scaled[...], axis=0, keepdims=True)
     gain_terms = jnp.concatenate(split(tiles(product, terms)), axis=0).astype(BF)
     out_ref[:, :, 2 * D :] = jnp.broadcast_to(gain_terms[None], (N, N, 128))
+    leaving[1].start()
+    for copy in leaving:
+        copy.wait()
 
 
 def rows_kernel(emb_ref, gain_ref, pick_ref, row_ref):
@@ -300,14 +309,14 @@
     gk_ref[:, 512:] = total[4:]
 
 
-def call(kernel, outs, ins, scratch=(), flops=0, moved=0, limit=16):
+def call(kernel, outs, ins, scratch=(), flops=0, moved=0, limit=16, far_out=False):
     far_space = pl.BlockSpec(memory_space=pl.ANY)
     vmem = pl.BlockSpec(memory_space=pltpu.VMEM)
     return pl.pallas_call(
         kernel,
         out_shape=[jax.ShapeDtypeStruct(shape, kind) for shape, kind in outs],
         in_specs=[far_space if far else vmem for _, far in ins],
-        out_specs=[vmem] * len(outs),
+        out_specs=[far_space if far_out else vmem] * len(outs),
         scratch_shapes=list(scratch),
         compiler_params=pltpu.CompilerParams(vmem_limit_bytes=limit * MIB),
         cost_estimate=pl.CostEstimate(flops=flops, bytes_accessed=moved, transcendentals=0),
@@ -339,11 +348,13 @@
             *[tall, tall],
             pltpu.VMEM((VOCAB, D), F32),
             pltpu.VMEM((8, 128), F32),
-            pltpu.SemaphoreType.DMA((11,)),
+            pltpu.VMEM((N, N, WIDE), BF),
+            pltpu.SemaphoreType.DMA((13,)),
         ],
         flops=8_000_000_000,
         moved=14_000_000,
         limit=56,
+        far_out=True,
     )
     parts = exchange(tables, "dp")
     embedding_later, _ = lax.optimization_barrier((embedding, tables))

time: 82.1 us -> 82 us (level)
  no operation moved by 1% of the time
where the time goes in v5:
time: 82 us; the launch traced here: 81.7 us
  starting transfers between devices  24.5 us (30%)
  blocking collectives  23.9 us (29%)
  Pallas kernels  16.7 us (20%)
  waiting for transfers between devices  14.9 us (18%)
  local copies, waits for them, and re-layouts  1.08 us (1%)
    all_to_all x1, blocking collectives, exchange(): return lax.all_to_all(value, axis, 0, 0, tiled=False)  23.9 us
    pallas_call x8, Pallas kernels, call(): pl.pallas_call(kernel, out_shape=[jax.ShapeDtypeStruct(shape, kind) for s...  16.7 us
    ppermute x5, starting transfers between devices, swap(): return lax.ppermute(value, 'seq', [(i, i ^ step) for i in range(N)])  12.4 us
    ppermute x5, waiting for transfers between devices, swap(): return lax.ppermute(value, 'seq', [(i, i ^ step) for i in range(N)])  9.05 us
    all_to_all x1, starting transfers between devices, exchange(): return lax.all_to_all(value, axis, 0, 0, tiled=False)  7.69 us
    all_to_all x1, waiting for transfers between devices, exchange(): return lax.all_to_all(value, axis, 0, 0, tiled=False)  4.94 us
    ppermute x1, starting transfers between devices, local(): prev_ids = lax.ppermute(byte_ids, 'seq', [(i, i + 1) for i in range(N - 1)])  4.37 us
  transfers between devices with their start and end apart: 7, of which 6 were waited for; matrix products, arithmetic and copies ran while one was open for 1% of the time, Pallas kernels for 1%

profile of v5, /device:TPU:1, one launch (start us, length us, event | category | flops | bytes accessed | tf_op | source)
XLA Modules:
  0.0 81.7 jit_solution(5725512684942430037)
XLA Ops:
  0.6 4.4 %collective-permute-start = (s32[1,256]{1,0:T(1,128)}, s32[1,256]{1,0:T(1,128)S(1)}, u32[]{:S(2)}, u32[]{:S(2)}) collective-permute-start(s32[1,256]{1,0:T(1,128)} %refs_2_.1), channel_id=1, source_target_pairs={{0,16},{16,32},{32,48},{48,64},{64,80},{80,96},{96,112},{112,128},... | collective-permute-start | bytes 3080 | tf_op jit(solution)/shard_map/ppermute | solution.py:328
  5.0 0.9 %collective-permute-done.refs_3_ = s32[1,256]{1,0:T(1,128)S(1)} collective-permute-done((s32[1,256]{1,0:T(1,128)}, s32[1,256]{1,0:T(1,128)S(1)}, u32[]{:S(2)}, u32[]{:S(2)}) %collective-permute-start) | collective-permute-done | bytes 1056 | tf_op jit(solution)/shard_map/ppermute | solution.py:328
  5.9 0.0 copy-start.2
  5.9 0.6 copy-done.2
  6.5 13.7 %shard_map.121 = bf16[16,16,2176]{2,1,0:T(8,128)(2,1)} custom-call(bf16[256,1024]{1,0:T(8,128)(2,1)} %emb_ref, f32[1,1024]{1,0:T(1,128)} %bitcast.4, s32[1,256]{1,0:T(1,128)} %refs_2_.1, s32[1,256]{1,0:T(1,128)} %copy-done.2, f32[2,512,128]{2,1,0:T(8,128)} %constant.4.clone.refs_4_, f32[2,16,128]{2,1,0:T(8,128)} %constant.5.clone.refs_5_, ...), custom_call_target="tpu_custom_call" | custom-call | flops 8000000000 | bytes 14000000 | tf_op jit(solution)/shard_map/pallas_call | solution.py:315
  20.2 0.0 copy-start
  20.2 0.0 copy-start.1
  20.3 23.9 %all_to_all.10.got_ref = bf16[16,16,2176]{2,1,0:T(8,128)(2,1)S(1)} all-to-all(bf16[16,16,2176]{2,1,0:T(8,128)(2,1)} %shard_map.121), channel_id=1, replica_groups=mesh['seq'=16,'dp'=16] {'dp'}, dimensions={0} | all-to-all | bytes 2228224 | tf_op jit(solution)/shard_map/all_to_all | solution.py:30
  44.1 0.2 shard_map.122
  44.4 2.1 %collective-permute-start.1 = (bf16[16,1408]{1,0:T(8,128)(2,1)S(1)}, bf16[16,1408]{1,0:T(8,128)(2,1)S(1)}, u32[]{:S(2)}, u32[]{:S(2)}) collective-permute-start(bf16[16,1408]{1,0:T(8,128)(2,1)S(1)} %get-tuple-element.21), channel_id=1, source_target_pairs={{0,16},{16,0},{32,48},{48,32},{64,80},{80,64},{96,112},{112,96},{1... | collective-permute-start | bytes 135176 | tf_op jit(solution)/shard_map/ppermute | solution.py:34
  46.4 3.9 %collective-permute-start.2 = (bf16[16,1408]{1,0:T(8,128)(2,1)S(1)}, bf16[16,1408]{1,0:T(8,128)(2,1)S(1)}, u32[]{:S(2)}, u32[]{:S(2)}) collective-permute-start(bf16[16,1408]{1,0:T(8,128)(2,1)S(1)} %get-tuple-element.22), channel_id=1, source_target_pairs={{0,32},{16,48},{32,0},{48,16},{64,96},{80,112},{96,64},{112,80},{1... | collective-permute-start | bytes 135176 | tf_op jit(solution)/shard_map/ppermute | solution.py:34
  50.3 0.1 collective-permute-start.3
  50.4 0.0 collective-permute-done.1.refs_0_
  50.4 1.6 %collective-permute-done.2.refs_1_ = bf16[16,1408]{1,0:T(8,128)(2,1)S(1)} collective-permute-done((bf16[16,1408]{1,0:T(8,128)(2,1)S(1)}, bf16[16,1408]{1,0:T(8,128)(2,1)S(1)}, u32[]{:S(2)}, u32[]{:S(2)}) %collective-permute-start.2) | collective-permute-done | bytes 45088 | tf_op jit(solution)/shard_map/ppermute | solution.py:34
  52.0 3.0 %collective-permute-done.3.refs_2_ = bf16[16,1408]{1,0:T(8,128)(2,1)S(1)} collective-permute-done((bf16[16,1408]{1,0:T(8,128)(2,1)S(1)}, bf16[16,1408]{1,0:T(8,128)(2,1)S(1)}, u32[]{:S(2)}, u32[]{:S(2)}) %collective-permute-start.3) | collective-permute-done | bytes 45088 | tf_op jit(solution)/shard_map/ppermute | solution.py:34
  55.0 2.8 %collective-permute-start.4 = (bf16[16,1280]{1,0:T(8,128)(2,1)S(1)}, bf16[16,1280]{1,0:T(8,128)(2,1)S(1)}, u32[]{:S(2)}, u32[]{:S(2)}) collective-permute-start(bf16[16,1280]{1,0:T(8,128)(2,1)S(1)} %get-tuple-element.26), channel_id=1, source_target_pairs={{0,128},{16,144},{32,160},{48,176},{64,192},{80,208},{96,224},{112... | collective-permute-start | bytes 122888 | tf_op jit(solution)/shard_map/ppermute | solution.py:34
  57.8 1.6 %collective-permute-done.4.refs_0_ = bf16[16,1280]{1,0:T(8,128)(2,1)S(1)} collective-permute-done((bf16[16,1280]{1,0:T(8,128)(2,1)S(1)}, bf16[16,1280]{1,0:T(8,128)(2,1)S(1)}, u32[]{:S(2)}, u32[]{:S(2)}) %collective-permute-start.4) | collective-permute-done | bytes 40992 | tf_op jit(solution)/shard_map/ppermute | solution.py:34
  59.5 3.6 %collective-permute-start.5 = (bf16[16,1280]{1,0:T(8,128)(2,1)S(1)}, bf16[16,1280]{1,0:T(8,128)(2,1)S(1)}, u32[]{:S(2)}, u32[]{:S(2)}) collective-permute-start(bf16[16,1280]{1,0:T(8,128)(2,1)S(1)} %get-tuple-element.28), channel_id=1, source_target_pairs={{0,64},{16,80},{32,96},{48,112},{64,0},{80,16},{96,32},{112,48},{1... | collective-permute-start | bytes 122888 | tf_op jit(solution)/shard_map/ppermute | solution.py:34
  63.1 0.0 copy-done
  63.1 0.0 copy-done.1
  63.1 0.4 shard_map.125
  63.5 2.8 %collective-permute-done.5.refs_0_ = bf16[16,1280]{1,0:T(8,128)(2,1)S(1)} collective-permute-done((bf16[16,1280]{1,0:T(8,128)(2,1)S(1)}, bf16[16,1280]{1,0:T(8,128)(2,1)S(1)}, u32[]{:S(2)}, u32[]{:S(2)}) %collective-permute-start.5) | collective-permute-done | bytes 40992 | tf_op jit(solution)/shard_map/ppermute | solution.py:34
  66.3 0.9 %shard_map.126 = bf16[16,8,512]{2,1,0:T(8,128)(2,1)} custom-call(f32[16,1152]{1,0:T(8,128)S(1)} %get-tuple-element.27.keys_ref, bf16[16,1280]{1,0:T(8,128)(2,1)S(1)} %collective-permute-done.5.refs_0_, bf16[32,128]{1,0:T(8,128)(2,1)S(1)} %get-tuple-element.30.refs_1_), custom_call_target="tpu_custom_call" | custom-call | flops 10000000 | bytes 400000 | tf_op jit(solution)/shard_map/pallas_call | solution.py:315
  67.3 7.7 %all-to-all-start.1 = ((bf16[16,8,512]{2,1,0:T(8,128)(2,1)}), bf16[16,8,512]{2,1,0:T(8,128)(2,1)S(1)}, u32[]{:S(2)}, u32[]{:S(2)}) async-start(bf16[16,8,512]{2,1,0:T(8,128)(2,1)} %shard_map.126), calls=%async_computation.1 | async-start | bytes 262144 | tf_op jit(solution)/shard_map/all_to_all | solution.py:30
  75.0 0.7 shard_map.128
  75.7 0.5 slice_bitcast_fusion
  76.2 4.9 %all-to-all-done.1.got_ref = bf16[16,8,512]{2,1,0:T(8,128)(2,1)S(1)} async-done(((bf16[16,8,512]{2,1,0:T(8,128)(2,1)}), bf16[16,8,512]{2,1,0:T(8,128)(2,1)S(1)}, u32[]{:S(2)}, u32[]{:S(2)}) %all-to-all-start.1) | async-done | bytes 131104 | tf_op jit(solution)/shard_map/all_to_all | solution.py:30
  81.1 0.6 shard_map.127
  (2 shorter events, 0.1 us)
Async XLA Ops:
  0.6 5.3 %collective-permute-start = (s32[1,256]{1,0:T(1,128)}, s32[1,256]{1,0:T(1,128)S(1)}, u32[]{:S(2)}, u32[]{:S(2)}) collective-permute-start(s32[1,256]{1,0:T(1,128)} %refs_2_.1), channel_id=1, source_target_pairs={{0,16},{16,32},{32,48},{48,64},{64,80},{80,96},{96,112},{112,128},... | collective-permute-start | bytes 3080 | tf_op jit(solution)/shard_map/ppermute | solution.py:328
  5.9 0.6 copy-start.2
  20.2 42.9 %copy-start = (bf16[256,1024]{1,0:T(8,128)(2,1)S(1)}, bf16[256,1024]{1,0:T(8,128)(2,1)}, u32[]{:S(2)}) copy-start(bf16[256,1024]{1,0:T(8,128)(2,1)} %emb_ref) | copy-start | bytes 1572868
  20.2 42.8 %copy-start.1 = (f32[1024]{0:T(1024)S(1)}, f32[1024]{0:T(1024)}, u32[]{:S(2)}) copy-start(f32[1024]{0:T(1024)} %param.12) | copy-start | bytes 12292
  44.4 6.0 %collective-permute-start.1 = (bf16[16,1408]{1,0:T(8,128)(2,1)S(1)}, bf16[16,1408]{1,0:T(8,128)(2,1)S(1)}, u32[]{:S(2)}, u32[]{:S(2)}) collective-permute-start(bf16[16,1408]{1,0:T(8,128)(2,1)S(1)} %get-tuple-element.21), channel_id=1, source_target_pairs={{0,16},{16,0},{32,48},{48,32},{64,80},{80,64},{96,112},{112,96},{1... | collective-permute-start | bytes 135176 | tf_op jit(solution)/shard_map/ppermute | solution.py:34
  46.4 5.6 %collective-permute-start.2 = (bf16[16,1408]{1,0:T(8,128)(2,1)S(1)}, bf16[16,1408]{1,0:T(8,128)(2,1)S(1)}, u32[]{:S(2)}, u32[]{:S(2)}) collective-permute-start(bf16[16,1408]{1,0:T(8,128)(2,1)S(1)} %get-tuple-element.22), channel_id=1, source_target_pairs={{0,32},{16,48},{32,0},{48,16},{64,96},{80,112},{96,64},{112,80},{1... | collective-permute-start | bytes 135176 | tf_op jit(solution)/shard_map/ppermute | solution.py:34
  50.3 4.7 %collective-permute-start.3 = (bf16[16,1408]{1,0:T(8,128)(2,1)S(1)}, bf16[16,1408]{1,0:T(8,128)(2,1)S(1)}, u32[]{:S(2)}, u32[]{:S(2)}) collective-permute-start(bf16[16,1408]{1,0:T(8,128)(2,1)S(1)} %get-tuple-element.23), channel_id=1, source_target_pairs={{0,48},{16,32},{32,16},{48,0},{64,112},{80,96},{96,80},{112,64},{1... | collective-permute-start | bytes 135176 | tf_op jit(solution)/shard_map/ppermute | solution.py:34
  55.0 4.4 %collective-permute-start.4 = (bf16[16,1280]{1,0:T(8,128)(2,1)S(1)}, bf16[16,1280]{1,0:T(8,128)(2,1)S(1)}, u32[]{:S(2)}, u32[]{:S(2)}) collective-permute-start(bf16[16,1280]{1,0:T(8,128)(2,1)S(1)} %get-tuple-element.26), channel_id=1, source_target_pairs={{0,128},{16,144},{32,160},{48,176},{64,192},{80,208},{96,224},{112... | collective-permute-start | bytes 122888 | tf_op jit(solution)/shard_map/ppermute | solution.py:34
  59.5 6.8 %collective-permute-start.5 = (bf16[16,1280]{1,0:T(8,128)(2,1)S(1)}, bf16[16,1280]{1,0:T(8,128)(2,1)S(1)}, u32[]{:S(2)}, u32[]{:S(2)}) collective-permute-start(bf16[16,1280]{1,0:T(8,128)(2,1)S(1)} %get-tuple-element.28), channel_id=1, source_target_pairs={{0,64},{16,80},{32,96},{48,112},{64,0},{80,16},{96,32},{112,48},{1... | collective-permute-start | bytes 122888 | tf_op jit(solution)/shard_map/ppermute | solution.py:34
  67.3 13.8 %all-to-all-start.1 = ((bf16[16,8,512]{2,1,0:T(8,128)(2,1)}), bf16[16,8,512]{2,1,0:T(8,128)(2,1)S(1)}, u32[]{:S(2)}, u32[]{:S(2)}) async-start(bf16[16,8,512]{2,1,0:T(8,128)(2,1)} %shard_map.126), calls=%async_computation.1 | async-start | bytes 262144 | tf_op jit(solution)/shard_map/all_to_all | solution.py:30
